TPU v7x, 512 devices: a whole 4x8x8 slice. The times are simulated.
512 devices in a mesh: seq: 128 (over y, z, core), grp: 4 (over x).
Axes of the slice: x: 4, y: 8, z: 8, core: 2. Of those that a mesh axis runs over, the one named last changes fastest.
Arguments:
- queries: bfloat16 [32768, 4096], P('seq', 'grp'), parts along dimension 1, may hold values from -4.5 to 4.5
- keys: bfloat16 [32768, 512], P('seq', 'grp'), parts along dimension 1, may hold values from -4.5 to 4.5
- values: bfloat16 [32768, 512], P('seq', 'grp'), parts along dimension 1, may hold values from -4.5 to 4.5
- grad_out: bfloat16 [32768, 4096], P('seq', 'grp'), parts along dimension 1, may hold values from -6 to 6
- lengths: int32 [516], replicated, may hold values from 0 to 512, as said below
- assign: int32 [128, 2], replicated, may hold values from 0 to 255, as said below
Outputs:
- attn_out: bfloat16 [32768, 4096], P('seq', 'grp'), parts along dimension 1
- grad_queries: bfloat16 [32768, 4096], P('seq', 'grp'), parts along dimension 1
- grad_keys: bfloat16 [32768, 512], P('seq', 'grp'), parts along dimension 1
- grad_values: bfloat16 [32768, 512], P('seq', 'grp'), parts along dimension 1
There are 4 independent parts, one for each index of `grp`. A program takes and returns all parts, laid end to end along the dimension named above; an argument that names none is the same for every part. Nothing has to cross between parts.
Inputs may be any that keep to these rules, and one draw needn't show every extreme that they name: The lengths sum to 32768; all positive lengths come first and zeros after them; the longest is exactly 512. `assign`: row d names the two spans held by device d, in increasing order; devices 2p and 2p + 1 hold the spans 4p to 4p + 3 between them, each once.
All inputs are finite; a program needn't handle non-finite values.
Results may differ from a plain program's by a relative error of at most 0.03.
Values may be sent and summed in bfloat16 or wider, within the bound.
A program may use at most 64 MiB of HBM per device.

v0:
```python
import math

import jax
import jax.numpy as jnp
from jax import lax
from jax.sharding import PartitionSpec as P


def passed_along(block, axis, distance):
    devices = range(lax.axis_size(axis))
    route = [(i - distance, i) for i in devices if i - distance in devices]
    return lax.ppermute(block, axis, route)


def document_index(doc_ends, position):
    flat = position.reshape(-1)
    counted = jnp.sum((doc_ends[None, :] <= flat[:, None]).astype(jnp.int32), axis=1)
    return counted.reshape(position.shape)


def attend(query_block, dout_block, key_block, value_block, allowed, head_count):
    row_count = query_block.shape[0]
    head_dim = key_block.shape[1]
    inv_root = 1.0 / math.sqrt(head_dim)
    query3 = query_block.reshape(row_count, head_count, head_dim)
    dout3 = dout_block.reshape(row_count, head_count, head_dim)
    scores = (
        jnp.einsum("qhd,kd->hqk", query3, key_block, preferred_element_type=jnp.float32) * inv_root
    )
    scores = jnp.where(allowed[None], scores, -1e30)
    top = jnp.max(scores, axis=2, keepdims=True)
    log_total = top + jnp.log(jnp.sum(jnp.exp(scores - top), axis=2, keepdims=True))
    probs = jnp.exp(scores - log_total)
    probs_low = probs.astype(jnp.bfloat16)
    attn = jnp.einsum(
        "hqk,kd->qhd", probs_low, value_block, preferred_element_type=jnp.float32
    ).astype(jnp.bfloat16)
    delta = jnp.sum(dout3.astype(jnp.float32) * attn.astype(jnp.float32), axis=2)
    dprobs = jnp.einsum("qhd,kd->hqk", dout3, value_block, preferred_element_type=jnp.float32)
    dscores = (probs * (dprobs - jnp.transpose(delta)[:, :, None])).astype(jnp.bfloat16)
    grad_query = (
        jnp.einsum("hqk,kd->qhd", dscores, key_block, preferred_element_type=jnp.float32) * inv_root
    ).astype(jnp.bfloat16)
    grad_key = (
        jnp.einsum("hqk,qhd->kd", dscores, query3, preferred_element_type=jnp.float32) * inv_root
    )
    grad_value = jnp.einsum("hqk,qhd->kd", probs_low, dout3, preferred_element_type=jnp.float32)
    width = head_count * head_dim
    return (
        attn.reshape(row_count, width),
        grad_query.reshape(row_count, width),
        jnp.concatenate([grad_key, grad_value], axis=1),
    )


def shards(queries, keys, values, grad_out, lengths, assign):
    row_count, width = queries.shape
    head_dim = keys.shape[1]
    head_count = width // head_dim
    half_rows = row_count // 2
    device_count = assign.shape[0]
    my_index = lax.axis_index("seq")
    is_odd = my_index % 2 == 1
    pair_base = my_index - my_index % 2
    doc_ends = jnp.cumsum(lengths)
    key_vals = jnp.concatenate([keys, values], axis=1)
    fetched = {0: key_vals}
    for offset in (-3, -2, -1, 1):
        fetched[offset] = passed_along(key_vals, "seq", -offset)
    even_window = jnp.concatenate([fetched[slot_index - 2] for slot_index in range(4)], axis=0)
    odd_window = jnp.concatenate([fetched[slot_index - 3] for slot_index in range(4)], axis=0)
    window = jnp.where(is_odd, odd_window, even_window)
    owners = pair_base - 2 + jnp.arange(4, dtype=jnp.int32)
    owner_valid = owners >= 0
    owner_match = owners[:, None] == jnp.arange(device_count, dtype=jnp.int32)[None, :]
    owner_rows = jnp.sum(jnp.where(owner_match[:, :, None], assign[None, :, :], 0), axis=1)
    window_ids = jnp.where(owner_valid[:, None], owner_rows, -100).reshape(-1)
    local_rows = jnp.arange(half_rows, dtype=jnp.int32)
    window_pos = window_ids[:, None] * half_rows + local_rows[None, :]
    window_doc = document_index(doc_ends, window_pos)
    window_doc = jnp.where((window_ids >= 0)[:, None], window_doc, -2)
    my_ids = lax.dynamic_slice_in_dim(assign, my_index, 1, 0)[0]
    partial_value = jnp.zeros((8, half_rows, 2 * head_dim), jnp.float32)
    attn_parts = []
    query_parts = []
    for half_index in range(2):
        query_id = my_ids[half_index]
        query_pos = query_id * half_rows + local_rows
        query_doc = document_index(doc_ends, query_pos)
        query_block = queries[half_index * half_rows : (half_index + 1) * half_rows]
        dout_block = grad_out[half_index * half_rows : (half_index + 1) * half_rows]
        flat_pos = window_pos.reshape(-1)
        flat_doc = window_doc.reshape(-1)
        allowed = (flat_doc[None, :] == query_doc[:, None]) & (
            flat_pos[None, :] <= query_pos[:, None]
        )
        attn, grad_query, grad_kv = attend(
            query_block, dout_block, window[:, :head_dim], window[:, head_dim:], allowed, head_count
        )
        partial_value = partial_value + grad_kv.reshape(8, half_rows, 2 * head_dim)
        attn_parts.append(attn)
        query_parts.append(grad_query)
    shard_parts = partial_value.reshape(4, row_count, 2 * head_dim)
    total = jnp.where(is_odd, shard_parts[3], shard_parts[2])
    empty_part = jnp.zeros((row_count, 2 * head_dim), jnp.float32)
    for offset in (-3, -2, -1, 1):
        even_slot = offset + 2
        odd_slot = offset + 3
        even_part = shard_parts[even_slot] if 0 <= even_slot <= 3 else empty_part
        odd_part = shard_parts[odd_slot] if 0 <= odd_slot <= 3 else empty_part
        outgoing = jnp.where(is_odd, odd_part, even_part)
        total = total + passed_along(outgoing.astype(jnp.bfloat16), "seq", offset).astype(
            outgoing.dtype
        )
    attn_out = jnp.concatenate(attn_parts, axis=0)
    grad_queries = jnp.concatenate(query_parts, axis=0)
    grad_keys = total[:, :head_dim].astype(jnp.bfloat16)
    grad_values = total[:, head_dim:].astype(jnp.bfloat16)
    return (attn_out, grad_queries, grad_keys, grad_values)


def solution(mesh):
    return jax.shard_map(
        shards,
        mesh=mesh,
        in_specs=(P("seq", "grp"), P("seq", "grp"), P("seq", "grp"), P("seq", "grp"), P(), P()),
        out_specs=(P("seq", "grp"), P("seq", "grp"), P("seq", "grp"), P("seq", "grp")),
        check_vma=False,
    )
```

profile of v0, /device:TPU:34, one launch (start us, length us, event | category | flops | bytes accessed | tf_op | source)
XLA Modules:
  0.0 70.0 jit_solution(3168763620220591410)
XLA Ops:
  0.6 0.9 %constant_dynamic-update-slice_fusion.1 = bf16[256,256]{1,0:T(8,128)(2,1)S(1)} fusion(bf16[256,128]{1,0:T(8,128)(2,1)} %param.7), kind=kLoop, calls=%fused_computation.49 | loop fusion | bytes 131072
  1.5 0.9 %constant_dynamic-update-slice_fusion = bf16[256,256]{1,0:T(8,128)(2,1)S(1)} fusion(bf16[256,256]{1,0:T(8,128)(2,1)S(1)} %constant_dynamic-update-slice_fusion.1, bf16[256,128]{1,0:T(8,128)(2,1)} %param.8), kind=kLoop, calls=%fused_computation.48 | loop fusion | bytes 131072 | tf_op jit(solution)/shard_map/concatenate | solution.py:66
  2.3 10.3 %collective-permute-start.3 = (bf16[256,256]{1,0:T(8,128)(2,1)S(1)}, bf16[256,256]{1,0:T(8,128)(2,1)S(1)}, u32[]{:S(2)}, u32[]{:S(2)}) collective-permute-start(bf16[256,256]{1,0:T(8,128)(2,1)S(1)} %constant_dynamic-update-slice_fusion), channel_id=1, source_target_pairs={{4,0},{8,4},{12,8},{16,12},{20,16},{24,20},{28,24},{32,28},{36,32}... | collective-permute-start | bytes 393224 | tf_op jit(solution)/shard_map/ppermute | solution.py:12
  12.6 1.9 %collective-permute-start.2 = (bf16[256,256]{1,0:T(8,128)(2,1)S(1)}, bf16[256,256]{1,0:T(8,128)(2,1)S(1)}, u32[]{:S(2)}, u32[]{:S(2)}) collective-permute-start(bf16[256,256]{1,0:T(8,128)(2,1)S(1)} %constant_dynamic-update-slice_fusion), channel_id=1, source_target_pairs={{0,4},{4,8},{8,12},{12,16},{16,20},{20,24},{24,28},{28,32},{32,36}... | collective-permute-start | bytes 393224 | tf_op jit(solution)/shard_map/ppermute | solution.py:12
  14.6 1.9 %collective-permute-start.1 = (bf16[256,256]{1,0:T(8,128)(2,1)S(1)}, bf16[256,256]{1,0:T(8,128)(2,1)S(1)}, u32[]{:S(2)}, u32[]{:S(2)}) collective-permute-start(bf16[256,256]{1,0:T(8,128)(2,1)S(1)} %constant_dynamic-update-slice_fusion), channel_id=1, source_target_pairs={{0,8},{4,12},{8,16},{12,20},{16,24},{20,28},{24,32},{28,36},{32,40... | collective-permute-start | bytes 393224 | tf_op jit(solution)/shard_map/ppermute | solution.py:12
  16.5 1.9 %collective-permute-start = (bf16[256,256]{1,0:T(8,128)(2,1)S(1)}, bf16[256,256]{1,0:T(8,128)(2,1)S(1)}, u32[]{:S(2)}, u32[]{:S(2)}) collective-permute-start(bf16[256,256]{1,0:T(8,128)(2,1)S(1)} %constant_dynamic-update-slice_fusion), channel_id=1, source_target_pairs={{0,12},{4,16},{8,20},{12,24},{16,28},{20,32},{24,36},{28,40},{32,4... | collective-permute-start | bytes 393224 | tf_op jit(solution)/shard_map/ppermute | solution.py:12
  23.7 1.1 %fusion.21 = (bf16[128,1024]{1,0:T(8,128)(2,1)S(1)}, bf16[128,1024]{1,0:T(8,128)(2,1)S(1)}) fusion(bf16[256,1024]{1,0:T(8,128)(2,1)} %param.6), kind=kLoop, calls=%fused_computation.68 | loop fusion | bytes 1048576 | tf_op jit(solution)/shard_map/slice | solution.py:90
  25.1 1.1 %fusion.20 = (bf16[128,1024]{1,0:T(8,128)(2,1)S(1)}, bf16[128,1024]{1,0:T(8,128)(2,1)S(1)}) fusion(bf16[256,1024]{1,0:T(8,128)(2,1)} %param.9), kind=kLoop, calls=%fused_computation.67 | loop fusion | bytes 1048576 | tf_op jit(solution)/shard_map/slice | solution.py:91
  27.4 1.6 %collective-permute-done = bf16[256,256]{1,0:T(8,128)(2,1)S(1)} collective-permute-done((bf16[256,256]{1,0:T(8,128)(2,1)S(1)}, bf16[256,256]{1,0:T(8,128)(2,1)S(1)}, u32[]{:S(2)}, u32[]{:S(2)}) %collective-permute-start) | collective-permute-done | bytes 131104 | tf_op jit(solution)/shard_map/ppermute | solution.py:12
  30.0 0.9 %exponential_reduce_fusion = f32[8,128]{1,0:T(8,128)S(1)} fusion(f32[1024,128,8]{1,0,2:T(8,128)S(1)} %get-tuple-element.33, f32[8,128]{1,0:T(8,128)S(1)} %get-tuple-element.32, pred[128,1024]{0,1:T(8,128)(4,1)S(1)} %get-tuple-element.29), kind=kLoop, calls=%fused_computation.9 | loop fusion | flops 4193280 | bytes 4333568 | tf_op jit(solution)/shard_map/reduce_sum | solution.py:32
  30.9 1.1 %multiply_reduce_fusion = (f32[128,8]{0,1:T(8,128)S(1)}, bf16[128,8,128]{2,0,1:T(8,128)(2,1)S(1)}) fusion(bf16[128,1024]{0,1:T(8,128)(2,1)S(1)} %copy.78, f32[1024,128,8]{1,0,2:T(8,128)S(1)} %get-tuple-element.33, f32[8,128]{1,0:T(8,128)S(1)} %log_add_fusion, pred[128,1024]{0,1:T(8,128)(4,1)S(1)} %get-tuple-element.29, ...), kind=kOutput, calls=%fused_computation.33 | convolution fusion | flops 273284096 | bytes 5120000 | tf_op jit(solution)/shard_map/hqk,kd->qhd/dot_general | solution.py:35
  32.0 2.0 %convolution_bitcast_fusion = f32[1024,128]{0,1:T(8,128)} fusion(bf16[128,8,128]{0,2,1:T(8,128)(2,1)S(1)} %bitcast.129, f32[1024,128,8]{1,0,2:T(8,128)S(1)} %get-tuple-element.33, f32[8,128]{1,0:T(8,128)S(1)} %log_add_fusion, pred[128,1024]{0,1:T(8,128)(4,1)S(1)} %get-tuple-element.29), kind=kOutput, calls=%fused_computation.17 | convolution fusion | flops 272629760 | bytes 5115904 | tf_op jit(solution)/shard_map/hqk,qhd->kd/dot_general | solution.py:47
  34.0 1.4 %fusion.1 = bf16[8,128,1024]{1,2,0:T(8,128)(2,1)S(1)} fusion(f32[1024,128,8]{1,0,2:T(8,128)S(1)} %get-tuple-element.33, bf16[128,8,128]{0,2,1:T(8,128)(2,1)S(1)} %bitcast.130, f32[8,128]{1,0:T(8,128)S(1)} %bitcast.135, f32[8,128]{1,0:T(8,128)S(1)} %log_add_fusion, pred[128,1024]{0,1:T(8,128)(4,1)S(1)} %get-tuple-element.29, ...), kind=kOutput, calls=%fused_computation.2 | convolution fusion | flops 274726912 | bytes 6955008 | tf_op jit(solution)/shard_map/qhd,kd->hqk/dot_general | solution.py:39
  37.5 0.9 %exponential_reduce_fusion.1 = f32[8,128]{1,0:T(8,128)S(1)} fusion(f32[1024,128,8]{1,0,2:T(8,128)S(1)} %get-tuple-element.35, f32[8,128]{1,0:T(8,128)S(1)} %get-tuple-element.34, pred[128,1024]{0,1:T(8,128)(4,1)S(1)} %get-tuple-element.28), kind=kLoop, calls=%fused_computation.11 | loop fusion | flops 4193280 | bytes 4333568 | tf_op jit(solution)/shard_map/reduce_sum | solution.py:32
  38.4 1.1 %multiply_reduce_fusion.1 = (f32[128,8]{0,1:T(8,128)S(1)}, bf16[128,8,128]{2,0,1:T(8,128)(2,1)S(1)}) fusion(bf16[128,1024]{0,1:T(8,128)(2,1)S(1)} %copy.74, f32[1024,128,8]{1,0,2:T(8,128)S(1)} %get-tuple-element.35, f32[8,128]{1,0:T(8,128)S(1)} %log_add_fusion.1, pred[128,1024]{0,1:T(8,128)(4,1)S(1)} %get-tuple-element.28, ...), kind=kOutput, calls=%fused_computation.34 | convolution fusion | flops 273284096 | bytes 5120000 | tf_op jit(solution)/shard_map/hqk,kd->qhd/dot_general | solution.py:35
  39.5 2.0 %convolution_bitcast_fusion.2 = f32[1024,128]{0,1:T(8,128)} fusion(bf16[128,8,128]{0,2,1:T(8,128)(2,1)S(1)} %bitcast.127, f32[1024,128,8]{1,0,2:T(8,128)S(1)} %get-tuple-element.35, f32[8,128]{1,0:T(8,128)S(1)} %log_add_fusion.1, pred[128,1024]{0,1:T(8,128)(4,1)S(1)} %get-tuple-element.28), kind=kOutput, calls=%fused_computation.20 | convolution fusion | flops 272629760 | bytes 5115904 | tf_op jit(solution)/shard_map/hqk,qhd->kd/dot_general | solution.py:47
  41.5 1.6 %fusion.3 = bf16[8,128,1024]{1,2,0:T(8,128)(2,1)S(1)} fusion(f32[1024,128,8]{1,0,2:T(8,128)S(1)} %get-tuple-element.35, bf16[128,8,128]{0,2,1:T(8,128)(2,1)S(1)} %bitcast.128, f32[8,128]{1,0:T(8,128)S(1)} %bitcast.136, f32[8,128]{1,0:T(8,128)S(1)} %log_add_fusion.1, pred[128,1024]{0,1:T(8,128)(4,1)S(1)} %get-tuple-element.28, ...), kind=kOutput, calls=%fused_computation.5 | convolution fusion | flops 274726912 | bytes 6955008 | tf_op jit(solution)/shard_map/qhd,kd->hqk/dot_general | solution.py:39
  44.7 1.4 %maximum_add_fusion = f32[1024,256]{0,1:T(8,128)S(1)} fusion(f32[1024,128]{0,1:T(8,128)} %convolution_bitcast_fusion.2, f32[1024,128]{0,1:T(8,128)S(1)} %fusion.9, f32[1024,128]{0,1:T(8,128)} %convolution_bitcast_fusion, f32[1024,128]{0,1:T(8,128)S(1)} %fusion.8), kind=kLoop, calls=%fused_computation.29 | loop fusion | flops 786432 | bytes 3145728 | tf_op jit(solution)/shard_map/add | solution.py:100
  46.1 6.5 %collective-permute-start.4 = (bf16[256,256]{0,1:T(8,128)(2,1)S(1)}, bf16[256,256]{0,1:T(8,128)(2,1)S(1)}, u32[]{:S(2)}, u32[]{:S(2)}) collective-permute-start(bf16[256,256]{0,1:T(8,128)(2,1)S(1)} %get-tuple-element.18), channel_id=1, source_target_pairs={{12,0},{16,4},{20,8},{24,12},{28,16},{32,20},{36,24},{40,28},{44,3... | collective-permute-start | bytes 393224 | tf_op jit(solution)/shard_map/ppermute | solution.py:12
  52.7 2.5 %collective-permute-start.6 = (bf16[256,256]{0,1:T(8,128)(2,1)S(1)}, bf16[256,256]{0,1:T(8,128)(2,1)S(1)}, u32[]{:S(2)}, u32[]{:S(2)}) collective-permute-start(bf16[256,256]{0,1:T(8,128)(2,1)S(1)} %get-tuple-element.19), channel_id=1, source_target_pairs={{4,0},{8,4},{12,8},{16,12},{20,16},{24,20},{28,24},{32,28},{36,32}... | collective-permute-start | bytes 393224 | tf_op jit(solution)/shard_map/ppermute | solution.py:12
  55.2 3.6 %collective-permute-start.5 = (bf16[256,256]{0,1:T(8,128)(2,1)S(1)}, bf16[256,256]{0,1:T(8,128)(2,1)S(1)}, u32[]{:S(2)}, u32[]{:S(2)}) collective-permute-start(bf16[256,256]{0,1:T(8,128)(2,1)S(1)} %get-tuple-element.20), channel_id=1, source_target_pairs={{8,0},{12,4},{16,8},{20,12},{24,16},{28,20},{32,24},{36,28},{40,32... | collective-permute-start | bytes 393224 | tf_op jit(solution)/shard_map/ppermute | solution.py:12
  58.8 1.9 %collective-permute-start.7 = (bf16[256,256]{0,1:T(8,128)(2,1)S(1)}, bf16[256,256]{0,1:T(8,128)(2,1)S(1)}, u32[]{:S(2)}, u32[]{:S(2)}) collective-permute-start(bf16[256,256]{0,1:T(8,128)(2,1)S(1)} %get-tuple-element.21), channel_id=1, source_target_pairs={{0,4},{4,8},{8,12},{12,16},{16,20},{20,24},{24,28},{28,32},{32,36}... | collective-permute-start | bytes 393224 | tf_op jit(solution)/shard_map/ppermute | solution.py:12
  60.7 0.8 %pad_maximum_fusion = bf16[256,1024]{1,0:T(8,128)(2,1)} fusion(bf16[128,1024]{1,0:T(8,128)(2,1)S(1)} %copy.73, bf16[128,1024]{1,0:T(8,128)(2,1)S(1)} %copy.72), kind=kLoop, calls=%fused_computation.31 | loop fusion | flops 1048576 | bytes 1048576 | tf_op jit(solution)/shard_map/concatenate | solution.py:115
  62.7 5.7 %collective-permute-done.7 = bf16[256,256]{0,1:T(8,128)(2,1)S(1)} collective-permute-done((bf16[256,256]{0,1:T(8,128)(2,1)S(1)}, bf16[256,256]{0,1:T(8,128)(2,1)S(1)}, u32[]{:S(2)}, u32[]{:S(2)}) %collective-permute-start.7) | collective-permute-done | bytes 131104 | tf_op jit(solution)/shard_map/ppermute | solution.py:12
  (53 shorter events, 12.9 us)
Async XLA Ops:
  2.3 25.0 %collective-permute-start.3 = (bf16[256,256]{1,0:T(8,128)(2,1)S(1)}, bf16[256,256]{1,0:T(8,128)(2,1)S(1)}, u32[]{:S(2)}, u32[]{:S(2)}) collective-permute-start(bf16[256,256]{1,0:T(8,128)(2,1)S(1)} %constant_dynamic-update-slice_fusion), channel_id=1, source_target_pairs={{4,0},{8,4},{12,8},{16,12},{20,16},{24,20},{28,24},{32,28},{36,32}... | collective-permute-start | bytes 393224 | tf_op jit(solution)/shard_map/ppermute | solution.py:12
  12.6 14.8 %collective-permute-start.2 = (bf16[256,256]{1,0:T(8,128)(2,1)S(1)}, bf16[256,256]{1,0:T(8,128)(2,1)S(1)}, u32[]{:S(2)}, u32[]{:S(2)}) collective-permute-start(bf16[256,256]{1,0:T(8,128)(2,1)S(1)} %constant_dynamic-update-slice_fusion), channel_id=1, source_target_pairs={{0,4},{4,8},{8,12},{12,16},{16,20},{20,24},{24,28},{28,32},{32,36}... | collective-permute-start | bytes 393224 | tf_op jit(solution)/shard_map/ppermute | solution.py:12
  14.6 12.9 %collective-permute-start.1 = (bf16[256,256]{1,0:T(8,128)(2,1)S(1)}, bf16[256,256]{1,0:T(8,128)(2,1)S(1)}, u32[]{:S(2)}, u32[]{:S(2)}) collective-permute-start(bf16[256,256]{1,0:T(8,128)(2,1)S(1)} %constant_dynamic-update-slice_fusion), channel_id=1, source_target_pairs={{0,8},{4,12},{8,16},{12,20},{16,24},{20,28},{24,32},{28,36},{32,40... | collective-permute-start | bytes 393224 | tf_op jit(solution)/shard_map/ppermute | solution.py:12
  16.5 12.5 %collective-permute-start = (bf16[256,256]{1,0:T(8,128)(2,1)S(1)}, bf16[256,256]{1,0:T(8,128)(2,1)S(1)}, u32[]{:S(2)}, u32[]{:S(2)}) collective-permute-start(bf16[256,256]{1,0:T(8,128)(2,1)S(1)} %constant_dynamic-update-slice_fusion), channel_id=1, source_target_pairs={{0,12},{4,16},{8,20},{12,24},{16,28},{20,32},{24,36},{28,40},{32,4... | collective-permute-start | bytes 393224 | tf_op jit(solution)/shard_map/ppermute | solution.py:12
  46.1 16.6 %collective-permute-start.4 = (bf16[256,256]{0,1:T(8,128)(2,1)S(1)}, bf16[256,256]{0,1:T(8,128)(2,1)S(1)}, u32[]{:S(2)}, u32[]{:S(2)}) collective-permute-start(bf16[256,256]{0,1:T(8,128)(2,1)S(1)} %get-tuple-element.18), channel_id=1, source_target_pairs={{12,0},{16,4},{20,8},{24,12},{28,16},{32,20},{36,24},{40,28},{44,3... | collective-permute-start | bytes 393224 | tf_op jit(solution)/shard_map/ppermute | solution.py:12
  52.7 10.0 %collective-permute-start.6 = (bf16[256,256]{0,1:T(8,128)(2,1)S(1)}, bf16[256,256]{0,1:T(8,128)(2,1)S(1)}, u32[]{:S(2)}, u32[]{:S(2)}) collective-permute-start(bf16[256,256]{0,1:T(8,128)(2,1)S(1)} %get-tuple-element.19), channel_id=1, source_target_pairs={{4,0},{8,4},{12,8},{16,12},{20,16},{24,20},{28,24},{32,28},{36,32}... | collective-permute-start | bytes 393224 | tf_op jit(solution)/shard_map/ppermute | solution.py:12
  55.2 7.5 %collective-permute-start.5 = (bf16[256,256]{0,1:T(8,128)(2,1)S(1)}, bf16[256,256]{0,1:T(8,128)(2,1)S(1)}, u32[]{:S(2)}, u32[]{:S(2)}) collective-permute-start(bf16[256,256]{0,1:T(8,128)(2,1)S(1)} %get-tuple-element.20), channel_id=1, source_target_pairs={{8,0},{12,4},{16,8},{20,12},{24,16},{28,20},{32,24},{36,28},{40,32... | collective-permute-start | bytes 393224 | tf_op jit(solution)/shard_map/ppermute | solution.py:12
  58.8 9.6 %collective-permute-start.7 = (bf16[256,256]{0,1:T(8,128)(2,1)S(1)}, bf16[256,256]{0,1:T(8,128)(2,1)S(1)}, u32[]{:S(2)}, u32[]{:S(2)}) collective-permute-start(bf16[256,256]{0,1:T(8,128)(2,1)S(1)} %get-tuple-element.21), channel_id=1, source_target_pairs={{0,4},{4,8},{8,12},{12,16},{16,20},{20,24},{24,28},{28,32},{32,36}... | collective-permute-start | bytes 393224 | tf_op jit(solution)/shard_map/ppermute | solution.py:12
where the time goes:
time: 70.5 us; the launch traced here: 70 us
  starting transfers between devices  30.6 us (43%)
  matrix products  13.3 us (19%)
  local copies, waits for them, and re-layouts  9.11 us (13%)
  other arithmetic  7.35 us (10%)
  waiting for transfers between devices  7.32 us (10%)
  between operations  2.3 us (3%)
    ppermute x8, starting transfers between devices, passed_along(): return lax.ppermute(block, axis, route)  30.6 us
    ppermute x8, waiting for transfers between devices, passed_along(): return lax.ppermute(block, axis, route)  7.32 us
    dot_general x2, matrix products, attend(): jnp.einsum('hqk,qhd->kd', probs_low, dout3, preferred_element_type=jnp.fl...  3.97 us
    dot_general x2, matrix products, attend(): jnp.einsum('qhd,kd->hqk', dout3, value_block, preferred_element_type=jnp....  2.95 us
    unnamed x5, local copies, waits for them, and re-layouts  2.66 us
    dot_general x2, matrix products, attend(): jnp.einsum('hqk,kd->qhd', probs_low, value_block, preferred_element_type=...  2.23 us
    reduce_sum x2, other arithmetic, attend(): jnp.sum(jnp.exp(scores - top), axis=2, keepdims=True)  1.73 us
    dot_general x2, matrix products, attend(): jnp.einsum('hqk,qhd->kd', dscores, query3, preferred_element_type=jnp.flo...  1.63 us
  transfers between devices with their start and end apart: 8, of which 2 were waited for; matrix products, arithmetic and copies ran while one was open for 14% of the time, Pallas kernels for 0%

commit v1 on v0

v1 whole, which is shorter than its diff:
```python
import functools
import math

import jax
import jax.numpy as jnp
from jax import lax
from jax.experimental import pallas as pl
from jax.experimental.pallas import tpu as pltpu
from jax.sharding import PartitionSpec as P

MESH = pl.DeviceIdType.MESH
SPAN = 128
DIM = 128
REACH = 5
F32 = jnp.float32
BF16 = jnp.bfloat16
NT = (((1,), (1,)), ((), ()))
NN = (((1,), (0,)), ((), ()))


def dot(a, b, dims):
    return lax.dot_general(a, b, dims, preferred_element_type=F32)


def places(count):
    me = lax.axis_index("seq")
    core = lax.rem(me, 2)
    return me, core, me + 1 - 2 * core, lax.rem(me + 2, count), lax.rem(me + count - 2, count)


def greet(devices, grp):
    barrier = pltpu.get_barrier_semaphore()
    for device in devices:
        pl.semaphore_signal(barrier, inc=1, device_id=(device, grp), device_id_type=MESH)
    pl.semaphore_wait(barrier, len(devices))


def gather_kernel(
    count, keys, values, lens, assign, kwin, vwin, starts, padded, own_sem, far_send, far_recv,
    near_send, near_recv, relay_send, relay_recv,
):
    me, core, beside, after, before = places(count)
    grp = lax.axis_index("grp")
    greet((beside, after, before), grp)

    def remote(src, dst, send, recv, device):
        return pltpu.make_async_remote_copy(
            src_ref=src, dst_ref=dst, send_sem=send, recv_sem=recv,
            device_id=(device, grp), device_id_type=MESH,
        )

    arrays = ((keys, kwin), (values, vwin))
    far, near, relay, own = [], [], [], []
    for span in range(2):
        for which, (src, win) in enumerate(arrays):
            slot = 2 * span + which
            far.append(remote(
                src.at[span], win.at[2 * core + span], far_send.at[slot], far_recv.at[slot], after))
            relay.append(remote(
                win.at[2 * core + span], win.at[2 * core + span],
                relay_send.at[slot], relay_recv.at[slot], beside))
    for which, (src, win) in enumerate(arrays):
        mine = win.at[pl.ds(4 + 2 * core, 2)]
        near.append(remote(src, mine, near_send.at[which], near_recv.at[which], beside))
        own.append(pltpu.make_async_copy(src, mine, own_sem.at[which]))
    for copy in far + near + own:
        copy.start()

    docs = lens.shape[1]
    wide = padded.shape[1]
    padded[...] = jnp.zeros_like(padded)
    padded[0:1, 0:docs] = lens[...]
    length = padded[...]
    high = length >> 8
    low = length - (high << 8)
    row = lax.broadcasted_iota(jnp.int32, (8, wide), 0)
    both = jnp.where(row == 1, pltpu.roll(low, 1, 0), high).astype(F32).astype(BF16)
    until = lax.broadcasted_iota(jnp.int32, (wide, wide), 0)
    upto = lax.broadcasted_iota(jnp.int32, (wide, wide), 1)
    lower = jnp.where(upto <= until, 1.0, 0.0).astype(BF16)
    sums = dot(lower, both, NT)
    ends = sums[:, 0:1] * 256.0 + sums[:, 1:2]
    for half in range(2):
        base = assign[me, half] * SPAN
        pos = (base + lax.broadcasted_iota(jnp.int32, (1, SPAN), 1)).astype(F32)
        start = jnp.max(jnp.where(ends <= pos, ends, 0.0), axis=0, keepdims=True)
        starts[:, half * SPAN : (half + 1) * SPAN] = jnp.broadcast_to(
            start, (8, SPAN)).astype(jnp.int32)

    for slot in range(4):
        far[slot].wait_recv()
        relay[slot].start()
    for copy in own:
        copy.wait()
    for copy in near:
        copy.wait()
    for slot in range(4):
        far[slot].wait_send()
        relay[slot].wait()


def attend_kernel(
    count, assign, first, queries, dout, kwin, vwin, starts, attn, dqueries, mine, theirs,
    kblk, vblk, ktr, vtr, bias, dkey, dvalue, part,
):
    half = pl.program_id(0)
    me, core, _, _, _ = places(count)
    chip = me // 2
    prev = lax.rem(chip + count // 2 - 1, count // 2)
    wrapped = jnp.where(chip == 0, 2 * count, 0)
    ids = [assign[2 * prev + w // 2, w % 2] - wrapped for w in range(4)]
    ids += [assign[2 * chip + w // 2, w % 2] for w in range(4)]
    span = assign[me, half]
    slots = []
    for back in range(REACH):
        slot = jnp.int32(0)
        for w in range(8):
            slot = jnp.where(ids[w] == span - back, w, slot)
        slots.append(slot)
    needed = span - first[0, half * SPAN] // SPAN + 1
    root = 1.0 / math.sqrt(DIM)
    scale = root * math.log2(math.e)
    heads = queries.shape[1] // DIM

    @pl.when(half == 0)
    def _():
        part[...] = jnp.zeros_like(part)

    def window(back):
        rows = slice(back * SPAN, (back + 1) * SPAN)
        kb = kwin[slots[back]]
        vb = vwin[slots[back]]
        kblk[rows] = kb
        vblk[rows] = vb
        ktr[:, rows] = kb.T
        vtr[:, rows] = vb.T
        kpos = (span - back) * SPAN + lax.broadcasted_iota(jnp.int32, (SPAN, SPAN), 0)
        qpos = span * SPAN + lax.broadcasted_iota(jnp.int32, (SPAN, SPAN), 1)
        ok = (kpos >= starts[0:1, :]) & (kpos <= qpos)
        bias[rows] = jnp.where(ok, 0.0, -1e30)

    def pair(reach, group):
        rows = slice(0, reach * SPAN)
        cols = pl.ds(pl.multiple_of(group * 2 * DIM, 2 * DIM), 2 * DIM)
        q2 = queries[:, cols]
        g2 = dout[:, cols]
        qr = jnp.concatenate([q2[:, :DIM], q2[:, DIM:]], axis=0)
        gr = jnp.concatenate([g2[:, :DIM], g2[:, DIM:]], axis=0)
        mask = bias[rows]
        scores = dot(kblk[rows], qr, NT) * scale + jnp.concatenate([mask, mask], axis=1)
        top = jnp.max(scores, axis=0, keepdims=True)
        raw = jnp.exp2(scores - top)
        probs = raw * (1.0 / jnp.sum(raw, axis=0, keepdims=True))
        low = probs.astype(BF16)
        dprobs = dot(vblk[rows], gr, NT)
        delta = jnp.sum(probs * dprobs, axis=0, keepdims=True)
        ds = (probs * (dprobs - delta)).astype(BF16)
        out = dot(vtr[:, rows], low, NN)
        dq = dot(ktr[:, rows], ds, NN) * root
        attn[:, cols] = jnp.concatenate([out[:, :SPAN].T, out[:, SPAN:].T], axis=1).astype(BF16)
        dqueries[:, cols] = jnp.concatenate([dq[:, :SPAN].T, dq[:, SPAN:].T], axis=1).astype(BF16)
        return dot(ds, qr, NN), dot(low, gr, NN)

    for reach in range(1, REACH + 1):

        @pl.when(needed == reach)
        def _(reach=reach):
            rows = slice(0, reach * SPAN)
            for back in range(reach):
                window(back)

            def step(i, carry):
                dk, dv = pair(reach, 2 * i)
                dk2, dv2 = pair(reach, 2 * i + 1)
                dk = dk + dk2
                dv = dv + dv2

                @pl.when(i == 0)
                def _():
                    dkey[rows] = dk
                    dvalue[rows] = dv

                @pl.when(i > 0)
                def _():
                    dkey[rows] += dk
                    dvalue[rows] += dv

                return carry

            lax.fori_loop(0, heads // 4, step, 0)
            for back in range(reach):
                part[slots[back], :, 0:DIM] += dkey[back * SPAN : (back + 1) * SPAN] * root
                part[slots[back], :, DIM:] += dvalue[back * SPAN : (back + 1) * SPAN]

    @pl.when(half == 1)
    def _():
        for i in range(2):
            mine[i] = part[2 * core + i]
            mine[2 + i] = part[4 + 2 * core + i]
            theirs[i] = part[2 - 2 * core + i].astype(BF16)
            theirs[2 + i] = part[6 - 2 * core + i].astype(BF16)


def reduce_kernel(
    count, mine, theirs, dkeys, dvalues, near_buf, out_buf, far_buf, near_send, near_recv,
    far_send, far_recv,
):
    _, core, beside, after, before = places(count)
    grp = lax.axis_index("grp")
    greet((beside, after, before), grp)

    def remote(src, dst, send, recv, device):
        return pltpu.make_async_remote_copy(
            src_ref=src, dst_ref=dst, send_sem=send, recv_sem=recv,
            device_id=(device, grp), device_id_type=MESH,
        )

    near = [
        remote(theirs.at[i], near_buf.at[i], near_send.at[i], near_recv.at[i], beside)
        for i in range(4)
    ]
    far = [
        remote(out_buf.at[i], far_buf.at[i], far_send.at[i], far_recv.at[i], before)
        for i in range(2)
    ]
    for copy in near:
        copy.start()
    for i in range(2):
        near[i].wait_recv()
        out_buf[i] = (mine[i] + near_buf[i].astype(F32)).astype(BF16)
        far[i].start()
    for i in range(2):
        near[2 + i].wait_recv()
    for i in range(2):
        far[i].wait_recv()
        total = mine[2 + i] + near_buf[2 + i].astype(F32) + far_buf[i].astype(F32)
        dkeys[i] = total[:, 0:DIM].astype(BF16)
        dvalues[i] = total[:, DIM:].astype(BF16)
    for copy in near + far:
        copy.wait_send()


def shards(count, queries, keys, values, grad_out, lengths, assign):
    width = queries.shape[1]
    any_spec = pl.BlockSpec(memory_space=pl.ANY)
    vmem = pl.BlockSpec(memory_space=pltpu.VMEM)
    smem = pl.BlockSpec(memory_space=pltpu.SMEM)
    dma = pltpu.SemaphoreType.DMA
    docs = lengths.shape[0]
    wide = -(-docs // 128) * 128
    shape = jax.ShapeDtypeStruct
    kwin, vwin, starts = pl.pallas_call(
        functools.partial(gather_kernel, count),
        out_shape=(
            shape((8, SPAN, DIM), BF16),
            shape((8, SPAN, DIM), BF16),
            shape((8, 2 * SPAN), jnp.int32),
        ),
        in_specs=[any_spec, any_spec, vmem, smem],
        out_specs=(any_spec, any_spec, vmem),
        scratch_shapes=[
            pltpu.VMEM((8, wide), jnp.int32),
            dma((2,)), dma((4,)), dma((4,)), dma((2,)), dma((2,)), dma((4,)), dma((4,)),
        ],
        compiler_params=pltpu.CompilerParams(
            collective_id=0, has_side_effects=True, vmem_limit_bytes=16 * 2**20),
        name="gather",
    )(
        keys.reshape(2, SPAN, DIM), values.reshape(2, SPAN, DIM), lengths.reshape(1, docs), assign
    )

    rows = pl.BlockSpec((SPAN, width), lambda half: (half, 0))
    attn, dqueries, mine, theirs = pl.pallas_call(
        functools.partial(attend_kernel, count),
        grid=(2,),
        out_shape=(
            shape((2 * SPAN, width), BF16),
            shape((2 * SPAN, width), BF16),
            shape((4, SPAN, 2 * DIM), F32),
            shape((4, SPAN, 2 * DIM), BF16),
        ),
        in_specs=[
            smem, smem, rows, rows,
            pl.BlockSpec((8, SPAN, DIM), lambda half: (0, 0, 0)),
            pl.BlockSpec((8, SPAN, DIM), lambda half: (0, 0, 0)),
            pl.BlockSpec((8, SPAN), lambda half: (0, half)),
        ],
        out_specs=(
            rows, rows,
            pl.BlockSpec((4, SPAN, 2 * DIM), lambda half: (0, 0, 0)),
            pl.BlockSpec((4, SPAN, 2 * DIM), lambda half: (0, 0, 0)),
        ),
        scratch_shapes=[
            pltpu.VMEM((REACH * SPAN, DIM), BF16),
            pltpu.VMEM((REACH * SPAN, DIM), BF16),
            pltpu.VMEM((DIM, REACH * SPAN), BF16),
            pltpu.VMEM((DIM, REACH * SPAN), BF16),
            pltpu.VMEM((REACH * SPAN, SPAN), F32),
            pltpu.VMEM((REACH * SPAN, DIM), F32),
            pltpu.VMEM((REACH * SPAN, DIM), F32),
            pltpu.VMEM((8, SPAN, 2 * DIM), F32),
        ],
        compiler_params=pltpu.CompilerParams(
            dimension_semantics=("arbitrary",), vmem_limit_bytes=40 * 2**20),
        name="attend",
    )(assign, starts, queries, grad_out, kwin, vwin, starts)

    dkeys, dvalues = pl.pallas_call(
        functools.partial(reduce_kernel, count),
        out_shape=(shape((2, SPAN, DIM), BF16), shape((2, SPAN, DIM), BF16)),
        in_specs=[vmem, vmem],
        out_specs=(vmem, vmem),
        scratch_shapes=[
            pltpu.VMEM((4, SPAN, 2 * DIM), BF16),
            pltpu.VMEM((2, SPAN, 2 * DIM), BF16),
            pltpu.VMEM((2, SPAN, 2 * DIM), BF16),
            dma((4,)), dma((4,)), dma((2,)), dma((2,)),
        ],
        compiler_params=pltpu.CompilerParams(
            collective_id=1, has_side_effects=True, vmem_limit_bytes=16 * 2**20),
        name="reduce",
    )(mine, theirs)
    return (
        attn, dqueries, dkeys.reshape(2 * SPAN, DIM), dvalues.reshape(2 * SPAN, DIM))


def solution(mesh):
    split = P("seq", "grp")
    return jax.shard_map(
        functools.partial(shards, mesh.shape["seq"]),
        mesh=mesh,
        in_specs=(split, split, split, split, P(), P()),
        out_specs=(split, split, split, split),
        check_vma=False,
    )
```

time: 70.5 us -> 42.8 us (0.61)
  the two profiles are of different devices: /device:TPU:34 before, /device:TPU:1 now
where the time goes in v1:
time: 42.8 us; the launch traced here: 42.5 us
  Pallas kernels  36.1 us (84%)
  local copies, waits for them, and re-layouts  5.68 us (13%)
  between operations  0.68 us (2%)
    pallas_call x1, Pallas kernels, shards(): pl.pallas_call(functools.partial(gather_kernel, count), out_shape=(shape(...  20.8 us
    pallas_call x1, Pallas kernels, shards(): pl.pallas_call(functools.partial(attend_kernel, count), grid=(2,), out_sh...  7.94 us
    pallas_call x1, Pallas kernels, shards(): pl.pallas_call(functools.partial(reduce_kernel, count), out_shape=(shape(...  7.36 us
    unnamed x11, local copies, waits for them, and re-layouts  4.96 us

profile of v1, /device:TPU:1, one launch (start us, length us, event | category | flops | bytes accessed | tf_op | source)
XLA Modules:
  0.0 42.5 jit_solution(11830585941142837081)
XLA Ops:
  0.6 0.0 copy-start.2
  0.6 0.7 %reshape.25.lens = s32[1,516]{1,0:T(1,128)S(1)} reshape(s32[516]{0:T(1024)} %param.10) | data formatting | bytes 4128 | tf_op jit(solution)/shard_map/reshape | solution.py:269
  1.4 0.8 %copy.11.assign = s32[128,2]{1,0:T(8,128)S(1)} copy(s32[128,2]{0,1:T(2,128)} %param.11) | data formatting | bytes 2048 | tf_op args[5]
  2.1 0.0 copy-done.2
  2.2 0.0 copy-start.3
  2.2 0.8 %copy-done.3 = bf16[256,128]{1,0:T(8,128)(2,1)S(1)} copy-done((bf16[256,128]{1,0:T(8,128)(2,1)S(1)}, bf16[256,128]{1,0:T(8,128)(2,1)}, u32[]{:S(2)}) %copy-start.3) | copy-done | bytes 65560
  3.0 20.8 %gather.1 = (bf16[8,128,128]{2,1,0:T(8,128)(2,1)S(1)}, bf16[8,128,128]{2,1,0:T(8,128)(2,1)S(1)}, s32[8,256]{1,0:T(8,128)S(1)}) custom-call(bf16[2,128,128]{2,1,0:T(8,128)(2,1)S(1)} %bitcast.4, bf16[2,128,128]{2,1,0:T(8,128)(2,1)S(1)} %bitcast.5, s32[1,516]{1,0:T(1,128)S(1)} %reshape.25.lens, s32[128,2]{1,0:T(8,128)S(1)} %copy.11.assign), custom_call_target="tpu_custom_call" | custom-call | tf_op jit(solution)/shard_map/gather/pallas_call | solution.py:252
  23.8 0.0 copy-start
  23.8 1.0 %copy-done = bf16[256,1024]{1,0:T(8,128)(2,1)S(1)} copy-done((bf16[256,1024]{1,0:T(8,128)(2,1)S(1)}, bf16[256,1024]{1,0:T(8,128)(2,1)}, u32[]{:S(2)}) %copy-start) | copy-done | bytes 524312
  24.9 0.0 copy-start.1
  24.9 1.0 %copy-done.1 = bf16[256,1024]{1,0:T(8,128)(2,1)S(1)} copy-done((bf16[256,1024]{1,0:T(8,128)(2,1)S(1)}, bf16[256,1024]{1,0:T(8,128)(2,1)}, u32[]{:S(2)}) %copy-start.1) | copy-done | bytes 524312
  25.9 7.9 %attend.1 = (bf16[256,1024]{1,0:T(8,128)(2,1)}, bf16[256,1024]{1,0:T(8,128)(2,1)}, f32[4,128,256]{2,1,0:T(8,128)S(1)}, bf16[4,128,256]{2,1,0:T(8,128)(2,1)S(1)}) custom-call(s32[128,2]{1,0:T(8,128)S(1)} %copy.11.assign, s32[8,256]{1,0:T(8,128)S(1)} %get-tuple-element.13.first.starts, bf16[256,1024]{1,0:T(8,128)(2,1)S(1)} %copy-done, ...), custom_call_target="tpu_custom_call" | custom-call | tf_op jit(solution)/shard_map/attend/pallas_call | solution.py:273
  33.9 7.4 %reduce.1 = (bf16[2,128,128]{2,1,0:T(8,128)(2,1)S(1)}, bf16[2,128,128]{2,1,0:T(8,128)(2,1)S(1)}) custom-call(f32[4,128,256]{2,1,0:T(8,128)S(1)} %get-tuple-element.18.mine, bf16[4,128,256]{2,1,0:T(8,128)(2,1)S(1)} %get-tuple-element.19.theirs), custom_call_target="tpu_custom_call" | custom-call | tf_op jit(solution)/shard_map/reduce/pallas_call | solution.py:308
  41.2 0.6 %copy.14 = bf16[256,128]{1,0:T(8,128)(2,1)} copy(bf16[256,128]{1,0:T(8,128)(2,1)S(1)} %bitcast.7) | data formatting | bytes 131072
  41.9 0.6 %copy.15 = bf16[256,128]{1,0:T(8,128)(2,1)} copy(bf16[256,128]{1,0:T(8,128)(2,1)S(1)} %bitcast.6) | data formatting | bytes 131072
Async XLA Ops:
  0.6 1.5 %copy-start.2 = (bf16[256,128]{1,0:T(8,128)(2,1)S(1)}, bf16[256,128]{1,0:T(8,128)(2,1)}, u32[]{:S(2)}) copy-start(bf16[256,128]{1,0:T(8,128)(2,1)} %param.7) | copy-start | bytes 196612
  2.2 0.8 %copy-start.3 = (bf16[256,128]{1,0:T(8,128)(2,1)S(1)}, bf16[256,128]{1,0:T(8,128)(2,1)}, u32[]{:S(2)}) copy-start(bf16[256,128]{1,0:T(8,128)(2,1)} %param.8) | copy-start | bytes 196612
  23.8 1.0 %copy-start = (bf16[256,1024]{1,0:T(8,128)(2,1)S(1)}, bf16[256,1024]{1,0:T(8,128)(2,1)}, u32[]{:S(2)}) copy-start(bf16[256,1024]{1,0:T(8,128)(2,1)} %queries.1) | copy-start | bytes 1572868
  24.9 1.0 %copy-start.1 = (bf16[256,1024]{1,0:T(8,128)(2,1)S(1)}, bf16[256,1024]{1,0:T(8,128)(2,1)}, u32[]{:S(2)}) copy-start(bf16[256,1024]{1,0:T(8,128)(2,1)} %dout.1) | copy-start | bytes 1572868

commit v2 on v0

v2 whole, which is shorter than its diff:
```python
import functools
import math

import jax
import jax.numpy as jnp
from jax import lax
from jax.experimental import pallas as pl
from jax.experimental.pallas import tpu as pltpu
from jax.sharding import PartitionSpec as P

MESH = pl.DeviceIdType.MESH
SPAN = 128
DIM = 128
GROUP = 4
F32 = jnp.float32
BF16 = jnp.bfloat16
NT = (((1,), (1,)), ((), ()))
NN = (((1,), (0,)), ((), ()))
ROOT = 1.0 / math.sqrt(DIM)


def dot(a, b, dims):
    return lax.dot_general(a, b, dims, preferred_element_type=F32)


def pick(values, wanted):
    index = jnp.int32(0)
    for i, value in enumerate(values):
        index = jnp.where(value == wanted, i, index)
    return index


def twice(x):
    return jnp.concatenate([x, x], axis=1)


def spans(x):
    return x.reshape(x.shape[0] // SPAN, SPAN, x.shape[1])


def main_kernel(
    count, q, g, k, v, lens, assign, attn, dq, dk, dv,
    lens_v, assign_s, padded, qslot, gslot, kown, vown, kprev, vprev, qr, gr,
    ko, vo, kot, vot, kp, vp, kpt, vpt, bias, expo, dpo, pb, sb, oto, stat,
    part_p, part_o, sum_send, sum_near, far_send_buf, far_buf, own_send, own_near,
    oq_mine, oq_near0, oq_near1,
    loc_sem, far_ks, far_kr, far_vs, far_vr, rel_ks, rel_kr, rel_vs, rel_vr,
    near_s, near_r, p_s, p_r, f_s, f_r, o_s, o_r, oq_s, oq_r,
):
    me = lax.axis_index("seq")
    grp = lax.axis_index("grp")
    core = lax.rem(me, 2)
    other = 1 - core
    chip = me // 2
    beside = me + 1 - 2 * core
    has_prev = chip > 0
    has_next = chip < count // 2 - 1
    before = jnp.where(has_prev, me - 2, me)
    after = jnp.where(has_next, me + 2, me)
    width = q.shape[2] // 2
    pairs = width // (2 * DIM)

    def remote(src, dst, send, recv, device):
        return pltpu.make_async_remote_copy(
            src_ref=src, dst_ref=dst, send_sem=send, recv_sem=recv,
            device_id=(device, grp), device_id_type=MESH,
        )

    def columns(which):
        return pl.ds(pl.multiple_of(which * width, width), width)

    own_slots = pl.ds(2 * core, 2)
    local = [
        pltpu.make_async_copy(k, kown.at[own_slots], loc_sem.at[0]),
        pltpu.make_async_copy(v, vown.at[own_slots], loc_sem.at[1]),
        pltpu.make_async_copy(lens, lens_v, loc_sem.at[2]),
        pltpu.make_async_copy(assign, assign_s, loc_sem.at[3]),
        pltpu.make_async_copy(q.at[:, :, columns(core)], qslot.at[own_slots], loc_sem.at[4]),
        pltpu.make_async_copy(g.at[:, :, columns(core)], gslot.at[own_slots], loc_sem.at[5]),
    ]
    far_k = [remote(k.at[a], kprev.at[2 * core + a], far_ks.at[a], far_kr.at[a], after)
             for a in range(2)]
    far_v = [remote(v.at[a], vprev.at[2 * core + a], far_vs.at[a], far_vr.at[a], after)
             for a in range(2)]
    relay_k = [remote(kprev.at[2 * core + a], kprev.at[2 * core + a], rel_ks.at[a], rel_kr.at[a],
                      beside) for a in range(2)]
    relay_v = [remote(vprev.at[2 * core + a], vprev.at[2 * core + a], rel_vs.at[a], rel_vr.at[a],
                      beside) for a in range(2)]
    near = [
        remote(k, kown.at[own_slots], near_s.at[0], near_r.at[0], beside),
        remote(v, vown.at[own_slots], near_s.at[1], near_r.at[1], beside),
        remote(q.at[:, :, columns(other)], qslot.at[own_slots], near_s.at[2], near_r.at[2], beside),
        remote(g.at[:, :, columns(other)], gslot.at[own_slots], near_s.at[3], near_r.at[3], beside),
    ]

    barrier = pltpu.get_barrier_semaphore()
    pl.semaphore_signal(barrier, inc=1, device_id=(beside, grp), device_id_type=MESH)

    @pl.when(has_prev)
    def _():
        pl.semaphore_signal(barrier, inc=1, device_id=(before, grp), device_id_type=MESH)

    @pl.when(has_next)
    def _():
        pl.semaphore_signal(barrier, inc=1, device_id=(after, grp), device_id_type=MESH)

    for copy in local:
        copy.start()
    pl.semaphore_wait(
        barrier, 1 + has_prev.astype(jnp.int32) + has_next.astype(jnp.int32))

    @pl.when(has_next)
    def _():
        for copy in far_k + far_v:
            copy.start()

    for copy in near:
        copy.start()

    docs = lens_v.shape[0]
    wide = padded.shape[1]
    padded[...] = jnp.zeros_like(padded)
    local[2].wait()
    padded[0:1, 0:docs] = lens_v[...].reshape(1, docs)
    length = padded[...]
    high = length >> 8
    low = length - (high << 8)
    row8 = lax.broadcasted_iota(jnp.int32, (8, wide), 0)
    both = jnp.where(row8 == 1, pltpu.roll(low, 1, 0), high).astype(F32).astype(BF16)
    until = lax.broadcasted_iota(jnp.int32, (wide, wide), 0)
    upto = lax.broadcasted_iota(jnp.int32, (wide, wide), 1)
    lower = jnp.where(upto <= until, 1.0, 0.0).astype(BF16)
    sums = dot(lower, both, NT)
    base = chip * (GROUP * SPAN)
    ends = sums[:, 0:1] * 256.0 + sums[:, 1:2] - base.astype(F32)
    least = -base.astype(F32)
    key_row = lax.broadcasted_iota(jnp.int32, (SPAN, SPAN), 0).astype(F32)
    query_col = lax.broadcasted_iota(jnp.int32, (SPAN, SPAN), 1).astype(F32)
    for j in range(GROUP):
        pos = query_col[0:1] + float(j * SPAN)
        start = jnp.max(jnp.where(ends <= pos, ends, least), axis=0, keepdims=True)
        for b in range(GROUP + 1):
            key = b if b <= j else b - 1 - GROUP
            ok = key_row + float(key * SPAN) >= start
            if b == j:
                ok = ok & (key_row <= query_col)
            bias[j, b * SPAN : (b + 1) * SPAN] = jnp.where(ok, 0.0, -1e30)

    local[3].wait()
    back = jnp.maximum(chip - 1, 0)
    here = [assign_s[s % 2, 2 * chip + s // 2] & (GROUP - 1) for s in range(GROUP)]
    there = [assign_s[s % 2, 2 * back + s // 2] & (GROUP - 1) for s in range(GROUP)]
    for copy in (local[0], local[1], local[4], local[5]):
        copy.wait()
    for copy in near:
        copy.wait_recv()
    for j in range(GROUP):
        slot = pick(here, j)
        rows = slice(j * SPAN, (j + 1) * SPAN)
        kb = kown[slot]
        vb = vown[slot]
        ko[rows] = kb
        vo[rows] = vb
        kot[:, rows] = kb.T
        vot[:, rows] = vb.T
        qb = qslot[slot]
        gb = gslot[slot]
        for h in range(2 * pairs):
            qr[j, h * SPAN : (h + 1) * SPAN] = qb[:, h * DIM : (h + 1) * DIM]
            gr[j, h * SPAN : (h + 1) * SPAN] = gb[:, h * DIM : (h + 1) * DIM]

    scale = ROOT * math.log2(math.e)
    part_p[...] = jnp.zeros_like(part_p)
    part_o[...] = jnp.zeros_like(part_o)

    def heads(p):
        return pl.ds(pl.multiple_of(p * 2 * SPAN, 2 * SPAN), 2 * SPAN)

    def own_scores(p, carry):
        for j in range(GROUP):
            n = (j + 1) * SPAN
            qj = qr[j, heads(p)]
            gj = gr[j, heads(p)]
            s = dot(ko[0:n], qj, NT) * scale + twice(bias[j, 0:n])
            m = jnp.max(s, axis=0, keepdims=True)
            e = jnp.exp2(s - m)
            expo[p, j, 0:n] = e
            dp = dot(vo[0:n], gj, NT)
            dpo[p, j, 0:n] = dp
            stat[p, j, 0:1] = m
            stat[p, j, 1:2] = jnp.sum(e, axis=0, keepdims=True)
            stat[p, j, 2:3] = jnp.sum(e * dp, axis=0, keepdims=True)
            oto[p, j] = dot(vot[:, 0:n], e.astype(BF16), NN)
        return carry

    lax.fori_loop(0, pairs, own_scores, 0)

    @pl.when(has_prev)
    def _():
        for a in range(2):
            far_k[a].wait_recv()
            relay_k[a].start()
        for a in range(2):
            relay_k[a].wait_recv()

    @pl.when(jnp.logical_not(has_prev))
    def _():
        kprev[...] = jnp.zeros_like(kprev)
        vprev[...] = jnp.zeros_like(vprev)

    for i in range(GROUP):
        rows = slice(i * SPAN, (i + 1) * SPAN)
        kb = kprev[pick(there, i)]
        kp[rows] = kb
        kpt[:, rows] = kb.T

    def prev_scores(p, carry):
        for j in range(GROUP):
            at = (j + 1) * SPAN
            s = dot(kp[j * SPAN :], qr[j, heads(p)], NT) * scale + twice(bias[j, at:])
            mo = stat[p, j, 0:1]
            m = jnp.maximum(mo, jnp.max(s, axis=0, keepdims=True))
            e = jnp.exp2(s - m)
            shrink = jnp.exp2(mo - m)
            r = 1.0 / (stat[p, j, 1:2] * shrink + jnp.sum(e, axis=0, keepdims=True))
            expo[p, j, at:] = e * r
            stat[p, j, 3:4] = shrink * r
        return carry

    lax.fori_loop(0, pairs, prev_scores, 0)

    @pl.when(has_prev)
    def _():
        for a in range(2):
            far_v[a].wait_recv()
            relay_v[a].start()
        for a in range(2):
            relay_v[a].wait_recv()

    for i in range(GROUP):
        rows = slice(i * SPAN, (i + 1) * SPAN)
        vb = vprev[pick(there, i)]
        vp[rows] = vb
        vpt[:, rows] = vb.T

    def prev_grads(p, carry):
        for j in range(GROUP):
            at = (j + 1) * SPAN
            qj = qr[j, heads(p)]
            gj = gr[j, heads(p)]
            dp = dot(vp[j * SPAN :], gj, NT)
            pr = expo[p, j, at:]
            delta = stat[p, j, 3:4] * stat[p, j, 2:3] + jnp.sum(pr * dp, axis=0, keepdims=True)
            stat[p, j, 4:5] = delta
            ds = (pr * (dp - delta)).astype(BF16)
            low = pr.astype(BF16)
            pb[p, j, at:] = low
            sb[p, j, at:] = ds
            part_p[j:, :, 0:DIM] += spans(dot(ds, qj, NN) * ROOT)
            part_p[j:, :, DIM:] += spans(dot(low, gj, NN))
        return carry

    lax.fori_loop(0, pairs, prev_grads, 0)

    def mine_of(spans, a):
        return jnp.where(core == 0, spans[a], spans[2 + a])

    def theirs_of(spans, a):
        return jnp.where(core == 0, spans[2 + a], spans[a])

    swap_p = [remote(sum_send.at[a], sum_near.at[a], p_s.at[a], p_r.at[a], beside)
              for a in range(2)]
    far_p = [remote(far_send_buf.at[a], far_buf.at[a], f_s.at[a], f_r.at[a], before)
             for a in range(2)]
    for a in range(2):
        sum_send[a] = part_p[theirs_of(there, a)].astype(BF16)
        swap_p[a].start()

    oq_near = (oq_near0, oq_near1)
    swap_oq = [remote(oq_mine.at[p], oq_near[p], oq_s.at[p], oq_r.at[p], beside)
               for p in range(pairs)]

    def own_grads(p):
        for j in range(GROUP):
            n = (j + 1) * SPAN
            qj = qr[j, heads(p)]
            gj = gr[j, heads(p)]
            alpha = stat[p, j, 3:4]
            pr = expo[p, j, 0:n] * alpha
            ds = (pr * (dpo[p, j, 0:n] - stat[p, j, 4:5])).astype(BF16)
            low = pr.astype(BF16)
            part_o[0 : j + 1, :, 0:DIM] += spans(dot(ds, qj, NN) * ROOT)
            part_o[0 : j + 1, :, DIM:] += spans(dot(low, gj, NN))
            out = oto[p, j] * alpha + dot(vpt[:, j * SPAN :], pb[p, j, n:], NN)
            dqt = dot(kot[:, 0:n], ds, NN) + dot(kpt[:, j * SPAN :], sb[p, j, n:], NN)
            dqt = dqt * ROOT
            for h in range(2):
                cols = slice(h * DIM, (h + 1) * DIM)
                oq_mine[p, 0, j, :, cols] = out[:, cols].T.astype(BF16)
                oq_mine[p, 1, j, :, cols] = dqt[:, cols].T.astype(BF16)

    own_grads(0)
    swap_oq[0].start()

    for a in range(2):
        swap_p[a].wait_recv()
        far_send_buf[a] = (
            part_p[mine_of(there, a)] + sum_near[a].astype(F32)).astype(BF16)

        @pl.when(has_prev)
        def _(a=a):
            far_p[a].start()

    for p in range(1, pairs):
        own_grads(p)
        swap_oq[p].start()

    swap_o = [remote(own_send.at[a], own_near.at[a], o_s.at[a], o_r.at[a], beside)
              for a in range(2)]
    for a in range(2):
        own_send[a] = part_o[theirs_of(here, a)].astype(BF16)
        swap_o[a].start()

    for p in range(pairs):
        swap_oq[p].wait_recv()
        for a in range(2):
            j = mine_of(here, a)
            for half, source in ((core, oq_mine.at[p]), (other, oq_near[p])):
                cols = pl.ds(
                    pl.multiple_of(half * width + p * 2 * DIM, 2 * DIM), 2 * DIM)
                attn[a, :, cols] = source[0, j]
                dq[a, :, cols] = source[1, j]

    @pl.when(jnp.logical_not(has_next))
    def _():
        far_buf[...] = jnp.zeros_like(far_buf)

    for a in range(2):
        swap_o[a].wait_recv()

        @pl.when(has_next)
        def _(a=a):
            far_p[a].wait_recv()

        total = part_o[mine_of(here, a)] + own_near[a].astype(F32) + far_buf[a].astype(F32)
        dk[a] = total[:, 0:DIM].astype(BF16)
        dv[a] = total[:, DIM:].astype(BF16)

    for copy in near + swap_p + swap_oq + swap_o:
        copy.wait_send()

    @pl.when(has_next)
    def _():
        for copy in far_k + far_v:
            copy.wait_send()

    @pl.when(has_prev)
    def _():
        for copy in relay_k + relay_v + far_p:
            copy.wait_send()


def store_kernel(*refs):
    n = (len(refs) - 1) // 2
    copies = [
        pltpu.make_async_copy(refs[i], refs[n + i], refs[2 * n].at[i]) for i in range(n)
    ]
    for copy in copies:
        copy.start()
    for copy in copies:
        copy.wait()


def shards(count, queries, keys, values, grad_out, lengths, assign):
    width = queries.shape[1]
    half = width // 2
    pairs = half // (2 * DIM)
    docs = lengths.shape[0]
    wide = -(-docs // 128) * 128
    hbm = pl.BlockSpec(memory_space=pltpu.HBM)
    vmem = pl.BlockSpec(memory_space=pltpu.VMEM)
    dma = pltpu.SemaphoreType.DMA
    shape = jax.ShapeDtypeStruct
    keyed = GROUP * SPAN
    seen = keyed + SPAN
    outs = (
        shape((2, SPAN, width), BF16),
        shape((2, SPAN, width), BF16),
        shape((2, SPAN, DIM), BF16),
        shape((2, SPAN, DIM), BF16),
    )
    results = pl.pallas_call(
        functools.partial(main_kernel, count),
        out_shape=outs,
        in_specs=[hbm] * 6,
        out_specs=(vmem,) * 4,
        scratch_shapes=[
            pltpu.VMEM((docs,), jnp.int32),
            pltpu.SMEM(assign.shape[::-1], jnp.int32),
            pltpu.VMEM((8, wide), jnp.int32),
            pltpu.VMEM((GROUP, SPAN, half), BF16),
            pltpu.VMEM((GROUP, SPAN, half), BF16),
            pltpu.VMEM((GROUP, SPAN, DIM), BF16),
            pltpu.VMEM((GROUP, SPAN, DIM), BF16),
            pltpu.VMEM((GROUP, SPAN, DIM), BF16),
            pltpu.VMEM((GROUP, SPAN, DIM), BF16),
            pltpu.VMEM((GROUP, half, DIM), BF16),
            pltpu.VMEM((GROUP, half, DIM), BF16),
            pltpu.VMEM((keyed, DIM), BF16),
            pltpu.VMEM((keyed, DIM), BF16),
            pltpu.VMEM((DIM, keyed), BF16),
            pltpu.VMEM((DIM, keyed), BF16),
            pltpu.VMEM((keyed, DIM), BF16),
            pltpu.VMEM((keyed, DIM), BF16),
            pltpu.VMEM((DIM, keyed), BF16),
            pltpu.VMEM((DIM, keyed), BF16),
            pltpu.VMEM((GROUP, seen, SPAN), F32),
            pltpu.VMEM((pairs, GROUP, seen, 2 * SPAN), F32),
            pltpu.VMEM((pairs, GROUP, keyed, 2 * SPAN), F32),
            pltpu.VMEM((pairs, GROUP, seen, 2 * SPAN), BF16),
            pltpu.VMEM((pairs, GROUP, seen, 2 * SPAN), BF16),
            pltpu.VMEM((pairs, GROUP, DIM, 2 * SPAN), F32),
            pltpu.VMEM((pairs, GROUP, 8, 2 * SPAN), F32),
            pltpu.VMEM((GROUP, SPAN, 2 * DIM), F32),
            pltpu.VMEM((GROUP, SPAN, 2 * DIM), F32),
            pltpu.VMEM((2, SPAN, 2 * DIM), BF16),
            pltpu.VMEM((2, SPAN, 2 * DIM), BF16),
            pltpu.VMEM((2, SPAN, 2 * DIM), BF16),
            pltpu.VMEM((2, SPAN, 2 * DIM), BF16),
            pltpu.VMEM((2, SPAN, 2 * DIM), BF16),
            pltpu.VMEM((2, SPAN, 2 * DIM), BF16),
            pltpu.VMEM((pairs, 2, GROUP, SPAN, 2 * DIM), BF16),
            pltpu.VMEM((2, GROUP, SPAN, 2 * DIM), BF16),
            pltpu.VMEM((2, GROUP, SPAN, 2 * DIM), BF16),
            dma((6,)),
            dma((2,)), dma((2,)), dma((2,)), dma((2,)),
            dma((2,)), dma((2,)), dma((2,)), dma((2,)),
            dma((4,)), dma((4,)),
            dma((2,)), dma((2,)), dma((2,)), dma((2,)), dma((2,)), dma((2,)),
            dma((pairs,)), dma((pairs,)),
        ],
        compiler_params=pltpu.CompilerParams(
            collective_id=0, has_side_effects=True, vmem_limit_bytes=40 * 2**20),
        name="attend",
    )(*[
        pltpu.with_memory_space_constraint(x, pltpu.HBM)
        for x in (
            queries.reshape(2, SPAN, width), grad_out.reshape(2, SPAN, width),
            keys.reshape(2, SPAN, DIM), values.reshape(2, SPAN, DIM), lengths, assign.T,
        )
    ])
    results = pl.pallas_call(
        store_kernel,
        out_shape=outs,
        in_specs=[pl.BlockSpec(memory_space=pl.ANY)] * 4,
        out_specs=(hbm,) * 4,
        scratch_shapes=[dma((4,))],
        name="store",
    )(*results)
    return tuple(r.reshape(2 * SPAN, r.shape[2]) for r in results)


def solution(mesh):
    split = P("seq", "grp")
    return jax.shard_map(
        functools.partial(shards, mesh.shape["seq"]),
        mesh=mesh,
        in_specs=(split, split, split, split, P(), P()),
        out_specs=(split, split, split, split),
        check_vma=False,
    )
```

time: 70.5 us -> 67.5 us (0.957)
  the two profiles are of different devices: /device:TPU:34 before, /device:TPU:57 now
where the time goes in v2:
time: 67.5 us; the launch traced here: 67.3 us
  Pallas kernels  63.9 us (95%)
  local copies, waits for them, and re-layouts  2.81 us (4%)
    pallas_call x1, Pallas kernels, shards(): pl.pallas_call(store_kernel, out_shape=outs, in_specs=[pl.BlockSpec(memor...  36.9 us
    pallas_call x1, Pallas kernels, shards(): pl.pallas_call(functools.partial(main_kernel, count), out_shape=outs, in_...  27 us
    unnamed x8, local copies, waits for them, and re-layouts  2.81 us

profile of v2, /device:TPU:57, one launch (start us, length us, event | category | flops | bytes accessed | tf_op | source)
XLA Modules:
  0.0 67.3 jit_solution(11149844826288013744)
XLA Ops:
  0.6 27.0 %attend.1 = (bf16[2,128,1024]{2,1,0:T(8,128)(2,1)S(1)}, bf16[2,128,1024]{2,1,0:T(8,128)(2,1)S(1)}, bf16[2,128,128]{2,1,0:T(8,128)(2,1)S(1)}, bf16[2,128,128]{2,1,0:T(8,128)(2,1)S(1)}) custom-call(bf16[2,128,1024]{2,1,0:T(8,128)(2,1)} %bitcast.9, bf16[2,128,1024]{2,1,0:T(8,128)(2,1)} %bitcast.10, bf16[2,128,128]{2,1,0:T(8,128)(2,1)} %bitcast.11, ...), custom_call_target="tpu_custom_call" | custom-call | tf_op jit(solution)/shard_map/attend/pallas_call | solution.py:392
  27.6 0.0 copy-start
  27.7 0.8 %copy-done = bf16[2,128,1024]{2,1,0:T(8,128)(2,1)} copy-done((bf16[2,128,1024]{2,1,0:T(8,128)(2,1)}, bf16[2,128,1024]{2,1,0:T(8,128)(2,1)S(1)}, u32[]{:S(2)}) %copy-start) | copy-done | bytes 524312
  28.4 0.0 copy-start.1
  28.4 0.8 %copy-done.1 = bf16[2,128,1024]{2,1,0:T(8,128)(2,1)} copy-done((bf16[2,128,1024]{2,1,0:T(8,128)(2,1)}, bf16[2,128,1024]{2,1,0:T(8,128)(2,1)S(1)}, u32[]{:S(2)}) %copy-start.1) | copy-done | bytes 524312
  29.2 0.0 copy-start.2
  29.2 0.6 copy-done.2
  29.8 0.0 copy-start.3
  29.8 0.6 copy-done.3
  30.5 36.9 %store.1 = (bf16[2,128,1024]{2,1,0:T(8,128)(2,1)}, bf16[2,128,1024]{2,1,0:T(8,128)(2,1)}, bf16[2,128,128]{2,1,0:T(8,128)(2,1)}, bf16[2,128,128]{2,1,0:T(8,128)(2,1)}) custom-call(bf16[2,128,1024]{2,1,0:T(8,128)(2,1)} %copy-done, bf16[2,128,1024]{2,1,0:T(8,128)(2,1)} %copy-done.1, bf16[2,128,128]{2,1,0:T(8,128)(2,1)} %copy-done.2, bf16[2,128,128]{2,1,0:T(8,128)(2,1)} %copy-done.3), custom_call_target="tpu_custom_call" | custom-call | tf_op jit(solution)/shard_map/store/pallas_call | solution.py:452
Async XLA Ops:
  27.6 0.8 %copy-start = (bf16[2,128,1024]{2,1,0:T(8,128)(2,1)}, bf16[2,128,1024]{2,1,0:T(8,128)(2,1)S(1)}, u32[]{:S(2)}) copy-start(bf16[2,128,1024]{2,1,0:T(8,128)(2,1)S(1)} %get-tuple-element.12.refs_0_) | copy-start | bytes 1572868
  28.4 0.8 %copy-start.1 = (bf16[2,128,1024]{2,1,0:T(8,128)(2,1)}, bf16[2,128,1024]{2,1,0:T(8,128)(2,1)S(1)}, u32[]{:S(2)}) copy-start(bf16[2,128,1024]{2,1,0:T(8,128)(2,1)S(1)} %get-tuple-element.13.refs_1_) | copy-start | bytes 1572868
  29.2 0.6 copy-start.2
  29.8 0.6 copy-start.3

commit v3 on v2

--- a/solution.py
+++ b/solution.py
@@ -30,8 +30,8 @@
     return index
 
 
-def twice(x):
-    return jnp.concatenate([x, x], axis=1)
+def every_head(x, heads):
+    return jnp.concatenate([x] * heads, axis=1)
 
 
 def spans(x):
@@ -43,7 +43,7 @@
     lens_v, assign_s, padded, qslot, gslot, kown, vown, kprev, vprev, qr, gr,
     ko, vo, kot, vot, kp, vp, kpt, vpt, bias, expo, dpo, pb, sb, oto, stat,
     part_p, part_o, sum_send, sum_near, far_send_buf, far_buf, own_send, own_near,
-    oq_mine, oq_near0, oq_near1,
+    oq_mine, oq_near,
     loc_sem, far_ks, far_kr, far_vs, far_vr, rel_ks, rel_kr, rel_vs, rel_vr,
     near_s, near_r, p_s, p_r, f_s, f_r, o_s, o_r, oq_s, oq_r,
 ):
@@ -58,7 +58,7 @@
     before = jnp.where(has_prev, me - 2, me)
     after = jnp.where(has_next, me + 2, me)
     width = q.shape[2] // 2
-    pairs = width // (2 * DIM)
+    heads = width // DIM
 
     def remote(src, dst, send, recv, device):
         return pltpu.make_async_remote_copy(
@@ -165,7 +165,7 @@
         vot[:, rows] = vb.T
         qb = qslot[slot]
         gb = gslot[slot]
-        for h in range(2 * pairs):
+        for h in range(heads):
             qr[j, h * SPAN : (h + 1) * SPAN] = qb[:, h * DIM : (h + 1) * DIM]
             gr[j, h * SPAN : (h + 1) * SPAN] = gb[:, h * DIM : (h + 1) * DIM]
 
@@ -173,27 +173,26 @@
     part_p[...] = jnp.zeros_like(part_p)
     part_o[...] = jnp.zeros_like(part_o)
 
-    def heads(p):
-        return pl.ds(pl.multiple_of(p * 2 * SPAN, 2 * SPAN), 2 * SPAN)
-
-    def own_scores(p, carry):
-        for j in range(GROUP):
-            n = (j + 1) * SPAN
-            qj = qr[j, heads(p)]
-            gj = gr[j, heads(p)]
-            s = dot(ko[0:n], qj, NT) * scale + twice(bias[j, 0:n])
-            m = jnp.max(s, axis=0, keepdims=True)
-            e = jnp.exp2(s - m)
-            expo[p, j, 0:n] = e
-            dp = dot(vo[0:n], gj, NT)
-            dpo[p, j, 0:n] = dp
-            stat[p, j, 0:1] = m
-            stat[p, j, 1:2] = jnp.sum(e, axis=0, keepdims=True)
-            stat[p, j, 2:3] = jnp.sum(e * dp, axis=0, keepdims=True)
-            oto[p, j] = dot(vot[:, 0:n], e.astype(BF16), NN)
-        return carry
-
-    lax.fori_loop(0, pairs, own_scores, 0)
+    def masked(keys, j, rows):
+        return dot(keys, qr[j], NT) * scale + every_head(bias[j, rows], heads)
+
+    tops = []
+    for j in range(GROUP):
+        own = slice(0, (j + 1) * SPAN)
+        s = masked(ko[own], j, own)
+        expo[j, own] = s
+        tops.append(jnp.max(s, axis=0, keepdims=True))
+    for j in range(GROUP):
+        own = slice(0, (j + 1) * SPAN)
+        dpo[j, own] = dot(vo[own], gr[j], NT)
+    for j in range(GROUP):
+        own = slice(0, (j + 1) * SPAN)
+        e = jnp.exp2(expo[j, own] - tops[j])
+        expo[j, own] = e
+        stat[j, 0:1] = tops[j]
+        stat[j, 1:2] = jnp.sum(e, axis=0, keepdims=True)
+        stat[j, 2:3] = jnp.sum(e * dpo[j, own], axis=0, keepdims=True)
+        oto[j] = dot(vot[:, own], e.astype(BF16), NN)
 
     @pl.when(has_prev)
     def _():
@@ -214,20 +213,22 @@
         kp[rows] = kb
         kpt[:, rows] = kb.T
 
-    def prev_scores(p, carry):
-        for j in range(GROUP):
-            at = (j + 1) * SPAN
-            s = dot(kp[j * SPAN :], qr[j, heads(p)], NT) * scale + twice(bias[j, at:])
-            mo = stat[p, j, 0:1]
-            m = jnp.maximum(mo, jnp.max(s, axis=0, keepdims=True))
-            e = jnp.exp2(s - m)
-            shrink = jnp.exp2(mo - m)
-            r = 1.0 / (stat[p, j, 1:2] * shrink + jnp.sum(e, axis=0, keepdims=True))
-            expo[p, j, at:] = e * r
-            stat[p, j, 3:4] = shrink * r
-        return carry
-
-    lax.fori_loop(0, pairs, prev_scores, 0)
+    tops = []
+    for j in range(GROUP):
+        at = (j + 1) * SPAN
+        s = masked(kp[j * SPAN :], j, slice(at, None))
+        expo[j, at:] = s
+        tops.append(jnp.maximum(stat[j, 0:1], jnp.max(s, axis=0, keepdims=True)))
+    norms = []
+    alphas = []
+    for j in range(GROUP):
+        at = (j + 1) * SPAN
+        e = jnp.exp2(expo[j, at:] - tops[j])
+        expo[j, at:] = e
+        shrink = jnp.exp2(stat[j, 0:1] - tops[j])
+        r = 1.0 / (stat[j, 1:2] * shrink + jnp.sum(e, axis=0, keepdims=True))
+        norms.append(r)
+        alphas.append(shrink * r)
 
     @pl.when(has_prev)
     def _():
@@ -243,24 +244,21 @@
         vp[rows] = vb
         vpt[:, rows] = vb.T
 
-    def prev_grads(p, carry):
-        for j in range(GROUP):
-            at = (j + 1) * SPAN
-            qj = qr[j, heads(p)]
-            gj = gr[j, heads(p)]
-            dp = dot(vp[j * SPAN :], gj, NT)
-            pr = expo[p, j, at:]
-            delta = stat[p, j, 3:4] * stat[p, j, 2:3] + jnp.sum(pr * dp, axis=0, keepdims=True)
-            stat[p, j, 4:5] = delta
-            ds = (pr * (dp - delta)).astype(BF16)
-            low = pr.astype(BF16)
-            pb[p, j, at:] = low
-            sb[p, j, at:] = ds
-            part_p[j:, :, 0:DIM] += spans(dot(ds, qj, NN) * ROOT)
-            part_p[j:, :, DIM:] += spans(dot(low, gj, NN))
-        return carry
-
-    lax.fori_loop(0, pairs, prev_grads, 0)
+    for j in range(GROUP):
+        dpo[j, (j + 1) * SPAN :] = dot(vp[j * SPAN :], gr[j], NT)
+    deltas = []
+    for j in range(GROUP):
+        at = (j + 1) * SPAN
+        pr = expo[j, at:] * norms[j]
+        dp = dpo[j, at:]
+        delta = alphas[j] * stat[j, 2:3] + jnp.sum(pr * dp, axis=0, keepdims=True)
+        deltas.append(delta)
+        pb[j, at:] = pr.astype(BF16)
+        sb[j, at:] = (pr * (dp - delta)).astype(BF16)
+    for j in range(GROUP):
+        at = (j + 1) * SPAN
+        part_p[j:, :, 0:DIM] += spans(dot(sb[j, at:], qr[j], NN) * ROOT)
+        part_p[j:, :, DIM:] += spans(dot(pb[j, at:], gr[j], NN))
 
     def mine_of(spans, a):
         return jnp.where(core == 0, spans[a], spans[2 + a])
@@ -276,31 +274,29 @@
         sum_send[a] = part_p[theirs_of(there, a)].astype(BF16)
         swap_p[a].start()
 
-    oq_near = (oq_near0, oq_near1)
-    swap_oq = [remote(oq_mine.at[p], oq_near[p], oq_s.at[p], oq_r.at[p], beside)
-               for p in range(pairs)]
-
-    def own_grads(p):
-        for j in range(GROUP):
-            n = (j + 1) * SPAN
-            qj = qr[j, heads(p)]
-            gj = gr[j, heads(p)]
-            alpha = stat[p, j, 3:4]
-            pr = expo[p, j, 0:n] * alpha
-            ds = (pr * (dpo[p, j, 0:n] - stat[p, j, 4:5])).astype(BF16)
-            low = pr.astype(BF16)
-            part_o[0 : j + 1, :, 0:DIM] += spans(dot(ds, qj, NN) * ROOT)
-            part_o[0 : j + 1, :, DIM:] += spans(dot(low, gj, NN))
-            out = oto[p, j] * alpha + dot(vpt[:, j * SPAN :], pb[p, j, n:], NN)
-            dqt = dot(kot[:, 0:n], ds, NN) + dot(kpt[:, j * SPAN :], sb[p, j, n:], NN)
-            dqt = dqt * ROOT
-            for h in range(2):
-                cols = slice(h * DIM, (h + 1) * DIM)
-                oq_mine[p, 0, j, :, cols] = out[:, cols].T.astype(BF16)
-                oq_mine[p, 1, j, :, cols] = dqt[:, cols].T.astype(BF16)
+    swap_oq = [remote(oq_mine.at[j], oq_near.at[j], oq_s.at[j], oq_r.at[j], beside)
+               for j in range(GROUP)]
+
+    def own_grads(j):
+        own = slice(0, (j + 1) * SPAN)
+        at = (j + 1) * SPAN
+        pr = expo[j, own] * alphas[j]
+        ds = (pr * (dpo[j, own] - deltas[j])).astype(BF16)
+        low = pr.astype(BF16)
+        part_o[0 : j + 1, :, 0:DIM] += spans(dot(ds, qr[j], NN) * ROOT)
+        part_o[0 : j + 1, :, DIM:] += spans(dot(low, gr[j], NN))
+        out = oto[j] * alphas[j] + dot(vpt[:, j * SPAN :], pb[j, at:], NN)
+        dqt = dot(kot[:, own], ds, NN) + dot(kpt[:, j * SPAN :], sb[j, at:], NN)
+        out = out.astype(BF16)
+        dqt = (dqt * ROOT).astype(BF16)
+        for h in range(heads):
+            cols = slice(h * DIM, (h + 1) * DIM)
+            oq_mine[j, 0, :, cols] = out[:, cols].T
+            oq_mine[j, 1, :, cols] = dqt[:, cols].T
+        swap_oq[j].start()
 
     own_grads(0)
-    swap_oq[0].start()
+    own_grads(1)
 
     for a in range(2):
         swap_p[a].wait_recv()
@@ -311,9 +307,8 @@
         def _(a=a):
             far_p[a].start()
 
-    for p in range(1, pairs):
-        own_grads(p)
-        swap_oq[p].start()
+    own_grads(2)
+    own_grads(3)
 
     swap_o = [remote(own_send.at[a], own_near.at[a], o_s.at[a], o_r.at[a], beside)
               for a in range(2)]
@@ -321,15 +316,13 @@
         own_send[a] = part_o[theirs_of(here, a)].astype(BF16)
         swap_o[a].start()
 
-    for p in range(pairs):
-        swap_oq[p].wait_recv()
-        for a in range(2):
-            j = mine_of(here, a)
-            for half, source in ((core, oq_mine.at[p]), (other, oq_near[p])):
-                cols = pl.ds(
-                    pl.multiple_of(half * width + p * 2 * DIM, 2 * DIM), 2 * DIM)
-                attn[a, :, cols] = source[0, j]
-                dq[a, :, cols] = source[1, j]
+    for j in range(GROUP):
+        swap_oq[j].wait_recv()
+    for a in range(2):
+        j = mine_of(here, a)
+        for half, source in ((core, oq_mine), (other, oq_near)):
+            attn[a, :, columns(half)] = source[j, 0]
+            dq[a, :, columns(half)] = source[j, 1]
 
     @pl.when(jnp.logical_not(has_next))
     def _():
@@ -374,7 +367,6 @@
 def shards(count, queries, keys, values, grad_out, lengths, assign):
     width = queries.shape[1]
     half = width // 2
-    pairs = half // (2 * DIM)
     docs = lengths.shape[0]
     wide = -(-docs // 128) * 128
     hbm = pl.BlockSpec(memory_space=pltpu.HBM)
@@ -415,12 +407,12 @@
             pltpu.VMEM((DIM, keyed), BF16),
             pltpu.VMEM((DIM, keyed), BF16),
             pltpu.VMEM((GROUP, seen, SPAN), F32),
-            pltpu.VMEM((pairs, GROUP, seen, 2 * SPAN), F32),
-            pltpu.VMEM((pairs, GROUP, keyed, 2 * SPAN), F32),
-            pltpu.VMEM((pairs, GROUP, seen, 2 * SPAN), BF16),
-            pltpu.VMEM((pairs, GROUP, seen, 2 * SPAN), BF16),
-            pltpu.VMEM((pairs, GROUP, DIM, 2 * SPAN), F32),
-            pltpu.VMEM((pairs, GROUP, 8, 2 * SPAN), F32),
+            pltpu.VMEM((GROUP, seen, half), F32),
+            pltpu.VMEM((GROUP, seen, half), F32),
+            pltpu.VMEM((GROUP, seen, half), BF16),
+            pltpu.VMEM((GROUP, seen, half), BF16),
+            pltpu.VMEM((GROUP, DIM, half), F32),
+            pltpu.VMEM((GROUP, 8, half), F32),
             pltpu.VMEM((GROUP, SPAN, 2 * DIM), F32),
             pltpu.VMEM((GROUP, SPAN, 2 * DIM), F32),
             pltpu.VMEM((2, SPAN, 2 * DIM), BF16),
@@ -429,15 +421,14 @@
             pltpu.VMEM((2, SPAN, 2 * DIM), BF16),
             pltpu.VMEM((2, SPAN, 2 * DIM), BF16),
             pltpu.VMEM((2, SPAN, 2 * DIM), BF16),
-            pltpu.VMEM((pairs, 2, GROUP, SPAN, 2 * DIM), BF16),
-            pltpu.VMEM((2, GROUP, SPAN, 2 * DIM), BF16),
-            pltpu.VMEM((2, GROUP, SPAN, 2 * DIM), BF16),
+            pltpu.VMEM((GROUP, 2, SPAN, half), BF16),
+            pltpu.VMEM((GROUP, 2, SPAN, half), BF16),
             dma((6,)),
             dma((2,)), dma((2,)), dma((2,)), dma((2,)),
             dma((2,)), dma((2,)), dma((2,)), dma((2,)),
             dma((4,)), dma((4,)),
             dma((2,)), dma((2,)), dma((2,)), dma((2,)), dma((2,)), dma((2,)),
-            dma((pairs,)), dma((pairs,)),
+            dma((GROUP,)), dma((GROUP,)),
         ],
         compiler_params=pltpu.CompilerParams(
             collective_id=0, has_side_effects=True, vmem_limit_bytes=40 * 2**20),
@@ -452,11 +443,11 @@
     results = pl.pallas_call(
         store_kernel,
         out_shape=outs,
-        in_specs=[pl.BlockSpec(memory_space=pl.ANY)] * 4,
+        in_specs=[pl.BlockSpec(memory_space=pltpu.VMEM)] * 4,
         out_specs=(hbm,) * 4,
         scratch_shapes=[dma((4,))],
         name="store",
-    )(*results)
+    )(*[pltpu.with_memory_space_constraint(r, pltpu.VMEM) for r in results])
     return tuple(r.reshape(2 * SPAN, r.shape[2]) for r in results)
 
 

time: 67.5 us -> 27.2 us (0.40)
  Pallas kernels: 63.9 us -> 26.2 us
  local copies, waits for them, and re-layouts: 2.81 us -> 0 us
    pallas_call x1, Pallas kernels: 36.9 us -> 1.03 us  [shards(): pl.pallas_call(store_kernel, out_shape=outs, in_specs=[pl.BlockSpec(memor...]
    unnamed x8 -> x0, local copies, waits for them, and re-layouts: 2.81 us -> none
    pallas_call x1, Pallas kernels: 27 us -> 25.2 us  [shards(): pl.pallas_call(functools.partial(main_kernel, count), out_shape=outs, in_...]
where the time goes in v3:
time: 27.2 us; the launch traced here: 26.9 us
  Pallas kernels  26.2 us (96%)
  between operations  0.64 us (2%)
    pallas_call x1, Pallas kernels, shards(): pl.pallas_call(functools.partial(main_kernel, count), out_shape=outs, in_...  25.2 us
    pallas_call x1, Pallas kernels, shards(): pl.pallas_call(store_kernel, out_shape=outs, in_specs=[pl.BlockSpec(memor...  1.03 us

profile of v3, /device:TPU:57, one launch (start us, length us, event | category | flops | bytes accessed | tf_op | source)
XLA Modules:
  0.0 26.9 jit_solution(5804106820138946571)
XLA Ops:
  0.6 25.2 %attend.1 = (bf16[2,128,1024]{2,1,0:T(8,128)(2,1)S(1)}, bf16[2,128,1024]{2,1,0:T(8,128)(2,1)S(1)}, bf16[2,128,128]{2,1,0:T(8,128)(2,1)S(1)}, bf16[2,128,128]{2,1,0:T(8,128)(2,1)S(1)}) custom-call(bf16[2,128,1024]{2,1,0:T(8,128)(2,1)} %bitcast.9, bf16[2,128,1024]{2,1,0:T(8,128)(2,1)} %bitcast.10, bf16[2,128,128]{2,1,0:T(8,128)(2,1)} %bitcast.11, ...), custom_call_target="tpu_custom_call" | custom-call | tf_op jit(solution)/shard_map/attend/pallas_call | solution.py:384
  25.8 1.0 %store.1 = (bf16[2,128,1024]{2,1,0:T(8,128)(2,1)}, bf16[2,128,1024]{2,1,0:T(8,128)(2,1)}, bf16[2,128,128]{2,1,0:T(8,128)(2,1)}, bf16[2,128,128]{2,1,0:T(8,128)(2,1)}) custom-call(bf16[2,128,1024]{2,1,0:T(8,128)(2,1)S(1)} %get-tuple-element.12.refs_0_, bf16[2,128,1024]{2,1,0:T(8,128)(2,1)S(1)} %get-tuple-element.13.refs_1_, ...), custom_call_target="tpu_custom_call" | custom-call | tf_op jit(solution)/shard_map/store/pallas_call | solution.py:443

commit v4 on v3

--- a/solution.py
+++ b/solution.py
@@ -114,7 +114,7 @@
         for copy in far_k + far_v:
             copy.start()
 
-    for copy in near:
+    for copy in near[:2]:
         copy.start()
 
     docs = lens_v.shape[0]
@@ -146,6 +146,14 @@
                 ok = ok & (key_row <= query_col)
             bias[j, b * SPAN : (b + 1) * SPAN] = jnp.where(ok, 0.0, -1e30)
 
+    @pl.when(has_next)
+    def _():
+        for copy in far_k + far_v:
+            copy.wait_send()
+
+    for copy in near[2:]:
+        copy.start()
+
     local[3].wait()
     back = jnp.maximum(chip - 1, 0)
     here = [assign_s[s % 2, 2 * chip + s // 2] & (GROUP - 1) for s in range(GROUP)]
@@ -219,6 +227,13 @@
         s = masked(kp[j * SPAN :], j, slice(at, None))
         expo[j, at:] = s
         tops.append(jnp.maximum(stat[j, 0:1], jnp.max(s, axis=0, keepdims=True)))
+
+    @pl.when(has_prev)
+    def _():
+        for a in range(2):
+            far_v[a].wait_recv()
+            relay_v[a].start()
+
     norms = []
     alphas = []
     for j in range(GROUP):
@@ -232,9 +247,6 @@
 
     @pl.when(has_prev)
     def _():
-        for a in range(2):
-            far_v[a].wait_recv()
-            relay_v[a].start()
         for a in range(2):
             relay_v[a].wait_recv()
 
@@ -293,10 +305,8 @@
             cols = slice(h * DIM, (h + 1) * DIM)
             oq_mine[j, 0, :, cols] = out[:, cols].T
             oq_mine[j, 1, :, cols] = dqt[:, cols].T
-        swap_oq[j].start()
 
     own_grads(0)
-    own_grads(1)
 
     for a in range(2):
         swap_p[a].wait_recv()
@@ -307,8 +317,10 @@
         def _(a=a):
             far_p[a].start()
 
-    own_grads(2)
-    own_grads(3)
+    swap_oq[0].start()
+    for j in range(1, GROUP):
+        own_grads(j)
+        swap_oq[j].start()
 
     swap_o = [remote(own_send.at[a], own_near.at[a], o_s.at[a], o_r.at[a], beside)
               for a in range(2)]
@@ -341,11 +353,6 @@
 
     for copy in near + swap_p + swap_oq + swap_o:
         copy.wait_send()
-
-    @pl.when(has_next)
-    def _():
-        for copy in far_k + far_v:
-            copy.wait_send()
 
     @pl.when(has_prev)
     def _():

time: 27.2 us -> 28.9 us (1.062)
  Pallas kernels: 26.2 us -> 28.1 us
    pallas_call x1, Pallas kernels: 25.2 us -> 27.1 us  [shards(): pl.pallas_call(functools.partial(main_kernel, count), out_shape=outs, in_...]
where the time goes in v4:
time: 28.9 us; the launch traced here: 28.8 us
  Pallas kernels  28.1 us (97%)
  between operations  0.64 us (2%)
    pallas_call x1, Pallas kernels, shards(): pl.pallas_call(functools.partial(main_kernel, count), out_shape=outs, in_...  27.1 us
    pallas_call x1, Pallas kernels, shards(): pl.pallas_call(store_kernel, out_shape=outs, in_specs=[pl.BlockSpec(memor...  1.03 us

profile of v4, /device:TPU:57, one launch (start us, length us, event | category | flops | bytes accessed | tf_op | source)
XLA Modules:
  0.0 28.8 jit_solution(8017939328386620194)
XLA Ops:
  0.6 27.1 %attend.1 = (bf16[2,128,1024]{2,1,0:T(8,128)(2,1)S(1)}, bf16[2,128,1024]{2,1,0:T(8,128)(2,1)S(1)}, bf16[2,128,128]{2,1,0:T(8,128)(2,1)S(1)}, bf16[2,128,128]{2,1,0:T(8,128)(2,1)S(1)}) custom-call(bf16[2,128,1024]{2,1,0:T(8,128)(2,1)} %bitcast.9, bf16[2,128,1024]{2,1,0:T(8,128)(2,1)} %bitcast.10, bf16[2,128,128]{2,1,0:T(8,128)(2,1)} %bitcast.11, ...), custom_call_target="tpu_custom_call" | custom-call | tf_op jit(solution)/shard_map/attend/pallas_call | solution.py:391
  27.7 1.0 %store.1 = (bf16[2,128,1024]{2,1,0:T(8,128)(2,1)}, bf16[2,128,1024]{2,1,0:T(8,128)(2,1)}, bf16[2,128,128]{2,1,0:T(8,128)(2,1)}, bf16[2,128,128]{2,1,0:T(8,128)(2,1)}) custom-call(bf16[2,128,1024]{2,1,0:T(8,128)(2,1)S(1)} %get-tuple-element.12.refs_0_, bf16[2,128,1024]{2,1,0:T(8,128)(2,1)S(1)} %get-tuple-element.13.refs_1_, ...), custom_call_target="tpu_custom_call" | custom-call | tf_op jit(solution)/shard_map/store/pallas_call | solution.py:450

commit v5 on v3

--- a/solution.py
+++ b/solution.py
@@ -40,10 +40,10 @@
 
 def main_kernel(
     count, q, g, k, v, lens, assign, attn, dq, dk, dv,
-    lens_v, assign_s, padded, qslot, gslot, kown, vown, kprev, vprev, qr, gr,
+    lens_v, assign_s, padded, qslot, gslot, kown, vown, kprev, vprev, qr, gr, qt, gt,
     ko, vo, kot, vot, kp, vp, kpt, vpt, bias, expo, dpo, pb, sb, oto, stat,
     part_p, part_o, sum_send, sum_near, far_send_buf, far_buf, own_send, own_near,
-    oq_mine, oq_near,
+    o_mine, o_near, q_mine, q_near,
     loc_sem, far_ks, far_kr, far_vs, far_vr, rel_ks, rel_kr, rel_vs, rel_vr,
     near_s, near_r, p_s, p_r, f_s, f_r, o_s, o_r, oq_s, oq_r,
 ):
@@ -111,7 +111,7 @@
 
     @pl.when(has_next)
     def _():
-        for copy in far_k + far_v:
+        for copy in far_k:
             copy.start()
 
     for copy in near:
@@ -131,6 +131,12 @@
     upto = lax.broadcasted_iota(jnp.int32, (wide, wide), 1)
     lower = jnp.where(upto <= until, 1.0, 0.0).astype(BF16)
     sums = dot(lower, both, NT)
+
+    @pl.when(has_next)
+    def _():
+        for copy in far_v:
+            copy.start()
+
     base = chip * (GROUP * SPAN)
     ends = sums[:, 0:1] * 256.0 + sums[:, 1:2] - base.astype(F32)
     least = -base.astype(F32)
@@ -166,15 +172,18 @@
         qb = qslot[slot]
         gb = gslot[slot]
         for h in range(heads):
-            qr[j, h * SPAN : (h + 1) * SPAN] = qb[:, h * DIM : (h + 1) * DIM]
-            gr[j, h * SPAN : (h + 1) * SPAN] = gb[:, h * DIM : (h + 1) * DIM]
+            cols = slice(h * DIM, (h + 1) * DIM)
+            qr[j, cols] = qb[:, cols]
+            gr[j, cols] = gb[:, cols]
+            qt[j, :, cols] = qb[:, cols].T
+            gt[j, :, cols] = gb[:, cols].T
 
     scale = ROOT * math.log2(math.e)
     part_p[...] = jnp.zeros_like(part_p)
     part_o[...] = jnp.zeros_like(part_o)
 
     def masked(keys, j, rows):
-        return dot(keys, qr[j], NT) * scale + every_head(bias[j, rows], heads)
+        return dot(keys, qt[j], NN) * scale + every_head(bias[j, rows], heads)
 
     tops = []
     for j in range(GROUP):
@@ -184,14 +193,13 @@
         tops.append(jnp.max(s, axis=0, keepdims=True))
     for j in range(GROUP):
         own = slice(0, (j + 1) * SPAN)
-        dpo[j, own] = dot(vo[own], gr[j], NT)
+        dpo[j, own] = dot(vo[own], gt[j], NN)
     for j in range(GROUP):
         own = slice(0, (j + 1) * SPAN)
         e = jnp.exp2(expo[j, own] - tops[j])
         expo[j, own] = e
         stat[j, 0:1] = tops[j]
         stat[j, 1:2] = jnp.sum(e, axis=0, keepdims=True)
-        stat[j, 2:3] = jnp.sum(e * dpo[j, own], axis=0, keepdims=True)
         oto[j] = dot(vot[:, own], e.astype(BF16), NN)
 
     @pl.when(has_prev)
@@ -229,12 +237,20 @@
         r = 1.0 / (stat[j, 1:2] * shrink + jnp.sum(e, axis=0, keepdims=True))
         norms.append(r)
         alphas.append(shrink * r)
+        if j == 1:
+
+            @pl.when(has_prev)
+            def _():
+                for a in range(2):
+                    far_v[a].wait_recv()
+                    relay_v[a].start()
+
+    for j in range(GROUP):
+        at = (j + 1) * SPAN
+        pb[j, at:] = (expo[j, at:] * norms[j]).astype(BF16)
 
     @pl.when(has_prev)
     def _():
-        for a in range(2):
-            far_v[a].wait_recv()
-            relay_v[a].start()
         for a in range(2):
             relay_v[a].wait_recv()
 
@@ -244,21 +260,34 @@
         vp[rows] = vb
         vpt[:, rows] = vb.T
 
-    for j in range(GROUP):
-        dpo[j, (j + 1) * SPAN :] = dot(vp[j * SPAN :], gr[j], NT)
     deltas = []
-    for j in range(GROUP):
+
+    def finish_out(j):
+        out = oto[j] * alphas[j] + dot(vpt[:, j * SPAN :], pb[j, (j + 1) * SPAN :], NN)
+        deltas.append(jnp.sum(out * gt[j].astype(F32), axis=0, keepdims=True))
+        out = out.astype(BF16)
+        for h in range(heads):
+            cols = slice(h * DIM, (h + 1) * DIM)
+            o_mine[j, :, cols] = out[:, cols].T
+
+    def prev_dprobs(j):
+        return dot(vp[j * SPAN :], gt[j], NN)
+
+    def prev_grads(j, dp):
         at = (j + 1) * SPAN
-        pr = expo[j, at:] * norms[j]
-        dp = dpo[j, at:]
-        delta = alphas[j] * stat[j, 2:3] + jnp.sum(pr * dp, axis=0, keepdims=True)
-        deltas.append(delta)
-        pb[j, at:] = pr.astype(BF16)
-        sb[j, at:] = (pr * (dp - delta)).astype(BF16)
-    for j in range(GROUP):
-        at = (j + 1) * SPAN
-        part_p[j:, :, 0:DIM] += spans(dot(sb[j, at:], qr[j], NN) * ROOT)
+        ds = (expo[j, at:] * norms[j] * (dp - deltas[j])).astype(BF16)
+        sb[j, at:] = ds
+        part_p[j:, :, 0:DIM] += spans(dot(ds, qr[j], NN) * ROOT)
         part_p[j:, :, DIM:] += spans(dot(pb[j, at:], gr[j], NN))
+
+    finish_out(0)
+    dp = prev_dprobs(0)
+    for j in range(1, GROUP):
+        finish_out(j)
+        next_dp = prev_dprobs(j)
+        prev_grads(j - 1, dp)
+        dp = next_dp
+    prev_grads(GROUP - 1, dp)
 
     def mine_of(spans, a):
         return jnp.where(core == 0, spans[a], spans[2 + a])
@@ -274,28 +303,32 @@
         sum_send[a] = part_p[theirs_of(there, a)].astype(BF16)
         swap_p[a].start()
 
-    swap_oq = [remote(oq_mine.at[j], oq_near.at[j], oq_s.at[j], oq_r.at[j], beside)
+    swap_out = remote(o_mine, o_near, oq_s.at[GROUP], oq_r.at[GROUP], beside)
+    swap_dq = [remote(q_mine.at[j], q_near.at[j], oq_s.at[j], oq_r.at[j], beside)
                for j in range(GROUP)]
+    swap_out.start()
+
+    def own_dscores(j):
+        own = slice(0, (j + 1) * SPAN)
+        pr = expo[j, own] * alphas[j]
+        pb[j, own] = pr.astype(BF16)
+        sb[j, own] = (pr * (dpo[j, own] - deltas[j])).astype(BF16)
 
     def own_grads(j):
         own = slice(0, (j + 1) * SPAN)
         at = (j + 1) * SPAN
-        pr = expo[j, own] * alphas[j]
-        ds = (pr * (dpo[j, own] - deltas[j])).astype(BF16)
-        low = pr.astype(BF16)
-        part_o[0 : j + 1, :, 0:DIM] += spans(dot(ds, qr[j], NN) * ROOT)
-        part_o[0 : j + 1, :, DIM:] += spans(dot(low, gr[j], NN))
-        out = oto[j] * alphas[j] + dot(vpt[:, j * SPAN :], pb[j, at:], NN)
-        dqt = dot(kot[:, own], ds, NN) + dot(kpt[:, j * SPAN :], sb[j, at:], NN)
-        out = out.astype(BF16)
+        dqt = dot(kot[:, own], sb[j, own], NN) + dot(kpt[:, j * SPAN :], sb[j, at:], NN)
         dqt = (dqt * ROOT).astype(BF16)
         for h in range(heads):
             cols = slice(h * DIM, (h + 1) * DIM)
-            oq_mine[j, 0, :, cols] = out[:, cols].T
-            oq_mine[j, 1, :, cols] = dqt[:, cols].T
-        swap_oq[j].start()
-
+            q_mine[j, :, cols] = dqt[:, cols].T
+        part_o[0 : j + 1, :, 0:DIM] += spans(dot(sb[j, own], qr[j], NN) * ROOT)
+        part_o[0 : j + 1, :, DIM:] += spans(dot(pb[j, own], gr[j], NN))
+
+    own_dscores(0)
+    own_dscores(1)
     own_grads(0)
+    own_dscores(2)
     own_grads(1)
 
     for a in range(2):
@@ -307,8 +340,13 @@
         def _(a=a):
             far_p[a].start()
 
+    for j in range(2):
+        swap_dq[j].start()
+    own_dscores(3)
     own_grads(2)
+    swap_dq[2].start()
     own_grads(3)
+    swap_dq[3].start()
 
     swap_o = [remote(own_send.at[a], own_near.at[a], o_s.at[a], o_r.at[a], beside)
               for a in range(2)]
@@ -316,13 +354,17 @@
         own_send[a] = part_o[theirs_of(here, a)].astype(BF16)
         swap_o[a].start()
 
-    for j in range(GROUP):
-        swap_oq[j].wait_recv()
     for a in range(2):
         j = mine_of(here, a)
-        for half, source in ((core, oq_mine), (other, oq_near)):
-            attn[a, :, columns(half)] = source[j, 0]
-            dq[a, :, columns(half)] = source[j, 1]
+        attn[a, :, columns(core)] = o_mine[j]
+        dq[a, :, columns(core)] = q_mine[j]
+    swap_out.wait_recv()
+    for a in range(2):
+        attn[a, :, columns(other)] = o_near[mine_of(here, a)]
+    for j in range(GROUP):
+        swap_dq[j].wait_recv()
+    for a in range(2):
+        dq[a, :, columns(other)] = q_near[mine_of(here, a)]
 
     @pl.when(jnp.logical_not(has_next))
     def _():
@@ -339,7 +381,7 @@
         dk[a] = total[:, 0:DIM].astype(BF16)
         dv[a] = total[:, DIM:].astype(BF16)
 
-    for copy in near + swap_p + swap_oq + swap_o:
+    for copy in near + swap_p + [swap_out] + swap_dq + swap_o:
         copy.wait_send()
 
     @pl.when(has_next)
@@ -355,9 +397,12 @@
 
 def store_kernel(*refs):
     n = (len(refs) - 1) // 2
-    copies = [
-        pltpu.make_async_copy(refs[i], refs[n + i], refs[2 * n].at[i]) for i in range(n)
-    ]
+    sem = refs[2 * n]
+    copies = []
+    for i in range(n):
+        for a in range(2):
+            copies.append(
+                pltpu.make_async_copy(refs[i].at[a], refs[n + i].at[a], sem.at[len(copies)]))
     for copy in copies:
         copy.start()
     for copy in copies:
@@ -398,6 +443,8 @@
             pltpu.VMEM((GROUP, SPAN, DIM), BF16),
             pltpu.VMEM((GROUP, half, DIM), BF16),
             pltpu.VMEM((GROUP, half, DIM), BF16),
+            pltpu.VMEM((GROUP, DIM, half), BF16),
+            pltpu.VMEM((GROUP, DIM, half), BF16),
             pltpu.VMEM((keyed, DIM), BF16),
             pltpu.VMEM((keyed, DIM), BF16),
             pltpu.VMEM((DIM, keyed), BF16),
@@ -408,7 +455,7 @@
             pltpu.VMEM((DIM, keyed), BF16),
             pltpu.VMEM((GROUP, seen, SPAN), F32),
             pltpu.VMEM((GROUP, seen, half), F32),
-            pltpu.VMEM((GROUP, seen, half), F32),
+            pltpu.VMEM((GROUP, keyed, half), F32),
             pltpu.VMEM((GROUP, seen, half), BF16),
             pltpu.VMEM((GROUP, seen, half), BF16),
             pltpu.VMEM((GROUP, DIM, half), F32),
@@ -421,14 +468,16 @@
             pltpu.VMEM((2, SPAN, 2 * DIM), BF16),
             pltpu.VMEM((2, SPAN, 2 * DIM), BF16),
             pltpu.VMEM((2, SPAN, 2 * DIM), BF16),
-            pltpu.VMEM((GROUP, 2, SPAN, half), BF16),
-            pltpu.VMEM((GROUP, 2, SPAN, half), BF16),
+            pltpu.VMEM((GROUP, SPAN, half), BF16),
+            pltpu.VMEM((GROUP, SPAN, half), BF16),
+            pltpu.VMEM((GROUP, SPAN, half), BF16),
+            pltpu.VMEM((GROUP, SPAN, half), BF16),
             dma((6,)),
             dma((2,)), dma((2,)), dma((2,)), dma((2,)),
             dma((2,)), dma((2,)), dma((2,)), dma((2,)),
             dma((4,)), dma((4,)),
             dma((2,)), dma((2,)), dma((2,)), dma((2,)), dma((2,)), dma((2,)),
-            dma((GROUP,)), dma((GROUP,)),
+            dma((GROUP + 1,)), dma((GROUP + 1,)),
         ],
         compiler_params=pltpu.CompilerParams(
             collective_id=0, has_side_effects=True, vmem_limit_bytes=40 * 2**20),
@@ -445,7 +494,7 @@
         out_shape=outs,
         in_specs=[pl.BlockSpec(memory_space=pltpu.VMEM)] * 4,
         out_specs=(hbm,) * 4,
-        scratch_shapes=[dma((4,))],
+        scratch_shapes=[dma((8,))],
         name="store",
     )(*[pltpu.with_memory_space_constraint(r, pltpu.VMEM) for r in results])
     return tuple(r.reshape(2 * SPAN, r.shape[2]) for r in results)

time: 27.2 us -> 26.9 us (0.989)
  no operation moved by 1% of the time
where the time goes in v5:
time: 26.9 us; the launch traced here: 26.8 us
  Pallas kernels  26.2 us (97%)
  between operations  0.64 us (2%)
    pallas_call x1, Pallas kernels, shards(): pl.pallas_call(functools.partial(main_kernel, count), out_shape=outs, in_...  25.1 us
    pallas_call x1, Pallas kernels, shards(): pl.pallas_call(store_kernel, out_shape=outs, in_specs=[pl.BlockSpec(memor...  1.07 us

profile of v5, /device:TPU:57, one launch (start us, length us, event | category | flops | bytes accessed | tf_op | source)
XLA Modules:
  0.0 26.8 jit_solution(12359242780006853989)
XLA Ops:
  0.6 25.1 %attend.1 = (bf16[2,128,1024]{2,1,0:T(8,128)(2,1)S(1)}, bf16[2,128,1024]{2,1,0:T(8,128)(2,1)S(1)}, bf16[2,128,128]{2,1,0:T(8,128)(2,1)S(1)}, bf16[2,128,128]{2,1,0:T(8,128)(2,1)S(1)}) custom-call(bf16[2,128,1024]{2,1,0:T(8,128)(2,1)} %bitcast.9, bf16[2,128,1024]{2,1,0:T(8,128)(2,1)} %bitcast.10, bf16[2,128,128]{2,1,0:T(8,128)(2,1)} %bitcast.11, ...), custom_call_target="tpu_custom_call" | custom-call | tf_op jit(solution)/shard_map/attend/pallas_call | solution.py:429
  25.7 1.1 %store.1 = (bf16[2,128,1024]{2,1,0:T(8,128)(2,1)}, bf16[2,128,1024]{2,1,0:T(8,128)(2,1)}, bf16[2,128,128]{2,1,0:T(8,128)(2,1)}, bf16[2,128,128]{2,1,0:T(8,128)(2,1)}) custom-call(bf16[2,128,1024]{2,1,0:T(8,128)(2,1)S(1)} %get-tuple-element.12.refs_0_, bf16[2,128,1024]{2,1,0:T(8,128)(2,1)S(1)} %get-tuple-element.13.refs_1_, ...), custom_call_target="tpu_custom_call" | custom-call | tf_op jit(solution)/shard_map/store/pallas_call | solution.py:492

commit v6 on v5

--- a/solution.py
+++ b/solution.py
@@ -17,6 +17,7 @@
 NT = (((1,), (1,)), ((), ()))
 NN = (((1,), (0,)), ((), ()))
 ROOT = 1.0 / math.sqrt(DIM)
+PIECE = 32
 
 
 def dot(a, b, dims):
@@ -36,6 +37,10 @@
 
 def spans(x):
     return x.reshape(x.shape[0] // SPAN, SPAN, x.shape[1])
+
+
+def fold(x, reduce):
+    return reduce(x.reshape(x.shape[0] // 8, 8, x.shape[1]), axis=0)
 
 
 def main_kernel(
@@ -182,25 +187,37 @@
     part_p[...] = jnp.zeros_like(part_p)
     part_o[...] = jnp.zeros_like(part_o)
 
-    def masked(keys, j, rows):
-        return dot(keys, qt[j], NN) * scale + every_head(bias[j, rows], heads)
+    def scores(keys, j, first, n):
+        s = dot(keys, qt[j], NN)
+        top = None
+        for at in range(0, n, PIECE):
+            rows = slice(first + at, first + at + PIECE)
+            piece = s[at : at + PIECE] * scale + every_head(bias[j, rows], heads)
+            expo[j, rows] = piece
+            top = fold(piece, jnp.max) if top is None else jnp.maximum(top, fold(piece, jnp.max))
+        return jnp.max(top, axis=0, keepdims=True)
+
+    def exponentials(j, first, n, top, low=None):
+        total = None
+        for at in range(0, n, PIECE):
+            rows = slice(first + at, first + at + PIECE)
+            e = jnp.exp2(expo[j, rows] - top)
+            expo[j, rows] = e
+            if low is not None:
+                low[j, rows] = e.astype(BF16)
+            total = fold(e, jnp.sum) if total is None else total + fold(e, jnp.sum)
+        return jnp.sum(total, axis=0, keepdims=True)
 
     tops = []
     for j in range(GROUP):
-        own = slice(0, (j + 1) * SPAN)
-        s = masked(ko[own], j, own)
-        expo[j, own] = s
-        tops.append(jnp.max(s, axis=0, keepdims=True))
-    for j in range(GROUP):
-        own = slice(0, (j + 1) * SPAN)
-        dpo[j, own] = dot(vo[own], gt[j], NN)
-    for j in range(GROUP):
-        own = slice(0, (j + 1) * SPAN)
-        e = jnp.exp2(expo[j, own] - tops[j])
-        expo[j, own] = e
+        n = (j + 1) * SPAN
+        tops.append(scores(ko[0:n], j, 0, n))
+        dpo[j, 0:n] = dot(vo[0:n], gt[j], NN)
+    for j in range(GROUP):
+        n = (j + 1) * SPAN
         stat[j, 0:1] = tops[j]
-        stat[j, 1:2] = jnp.sum(e, axis=0, keepdims=True)
-        oto[j] = dot(vot[:, own], e.astype(BF16), NN)
+        stat[j, 1:2] = exponentials(j, 0, n, tops[j], pb)
+        oto[j] = dot(vot[:, 0:n], pb[j, 0:n], NN)
 
     @pl.when(has_prev)
     def _():
@@ -223,18 +240,14 @@
 
     tops = []
     for j in range(GROUP):
-        at = (j + 1) * SPAN
-        s = masked(kp[j * SPAN :], j, slice(at, None))
-        expo[j, at:] = s
-        tops.append(jnp.maximum(stat[j, 0:1], jnp.max(s, axis=0, keepdims=True)))
+        top = scores(kp[j * SPAN :], j, (j + 1) * SPAN, (GROUP - j) * SPAN)
+        tops.append(jnp.maximum(stat[j, 0:1], top))
     norms = []
     alphas = []
     for j in range(GROUP):
-        at = (j + 1) * SPAN
-        e = jnp.exp2(expo[j, at:] - tops[j])
-        expo[j, at:] = e
+        total = exponentials(j, (j + 1) * SPAN, (GROUP - j) * SPAN, tops[j])
         shrink = jnp.exp2(stat[j, 0:1] - tops[j])
-        r = 1.0 / (stat[j, 1:2] * shrink + jnp.sum(e, axis=0, keepdims=True))
+        r = 1.0 / (stat[j, 1:2] * shrink + total)
         norms.append(r)
         alphas.append(shrink * r)
         if j == 1:
@@ -246,8 +259,11 @@
                     relay_v[a].start()
 
     for j in range(GROUP):
-        at = (j + 1) * SPAN
-        pb[j, at:] = (expo[j, at:] * norms[j]).astype(BF16)
+        for at in range((j + 1) * SPAN, expo.shape[1], PIECE):
+            rows = slice(at, at + PIECE)
+            pr = expo[j, rows] * norms[j]
+            expo[j, rows] = pr
+            pb[j, rows] = pr.astype(BF16)
 
     @pl.when(has_prev)
     def _():
@@ -275,9 +291,10 @@
 
     def prev_grads(j, dp):
         at = (j + 1) * SPAN
-        ds = (expo[j, at:] * norms[j] * (dp - deltas[j])).astype(BF16)
-        sb[j, at:] = ds
-        part_p[j:, :, 0:DIM] += spans(dot(ds, qr[j], NN) * ROOT)
+        for p in range(0, dp.shape[0], PIECE):
+            rows = slice(at + p, at + p + PIECE)
+            sb[j, rows] = (expo[j, rows] * (dp[p : p + PIECE] - deltas[j])).astype(BF16)
+        part_p[j:, :, 0:DIM] += spans(dot(sb[j, at:], qr[j], NN) * ROOT)
         part_p[j:, :, DIM:] += spans(dot(pb[j, at:], gr[j], NN))
 
     finish_out(0)
@@ -309,10 +326,11 @@
     swap_out.start()
 
     def own_dscores(j):
-        own = slice(0, (j + 1) * SPAN)
-        pr = expo[j, own] * alphas[j]
-        pb[j, own] = pr.astype(BF16)
-        sb[j, own] = (pr * (dpo[j, own] - deltas[j])).astype(BF16)
+        for at in range(0, (j + 1) * SPAN, PIECE):
+            rows = slice(at, at + PIECE)
+            pr = expo[j, rows] * alphas[j]
+            pb[j, rows] = pr.astype(BF16)
+            sb[j, rows] = (pr * (dpo[j, rows] - deltas[j])).astype(BF16)
 
     def own_grads(j):
         own = slice(0, (j + 1) * SPAN)

time: 26.9 us -> 27 us (level)
  no operation moved by 1% of the time
where the time goes in v6:
time: 27 us; the launch traced here: 26.8 us
  Pallas kernels  26.2 us (97%)
  between operations  0.64 us (2%)
    pallas_call x1, Pallas kernels, shards(): pl.pallas_call(functools.partial(main_kernel, count), out_shape=outs, in_...  25.1 us
    pallas_call x1, Pallas kernels, shards(): pl.pallas_call(store_kernel, out_shape=outs, in_specs=[pl.BlockSpec(memor...  1.07 us

profile of v6, /device:TPU:57, one launch (start us, length us, event | category | flops | bytes accessed | tf_op | source)
XLA Modules:
  0.0 26.8 jit_solution(17701185462235814642)
XLA Ops:
  0.6 25.1 %attend.1 = (bf16[2,128,1024]{2,1,0:T(8,128)(2,1)S(1)}, bf16[2,128,1024]{2,1,0:T(8,128)(2,1)S(1)}, bf16[2,128,128]{2,1,0:T(8,128)(2,1)S(1)}, bf16[2,128,128]{2,1,0:T(8,128)(2,1)S(1)}) custom-call(bf16[2,128,1024]{2,1,0:T(8,128)(2,1)} %bitcast.9, bf16[2,128,1024]{2,1,0:T(8,128)(2,1)} %bitcast.10, bf16[2,128,128]{2,1,0:T(8,128)(2,1)} %bitcast.11, ...), custom_call_target="tpu_custom_call" | custom-call | tf_op jit(solution)/shard_map/attend/pallas_call | solution.py:447
  25.8 1.1 %store.1 = (bf16[2,128,1024]{2,1,0:T(8,128)(2,1)}, bf16[2,128,1024]{2,1,0:T(8,128)(2,1)}, bf16[2,128,128]{2,1,0:T(8,128)(2,1)}, bf16[2,128,128]{2,1,0:T(8,128)(2,1)}) custom-call(bf16[2,128,1024]{2,1,0:T(8,128)(2,1)S(1)} %get-tuple-element.12.refs_0_, bf16[2,128,1024]{2,1,0:T(8,128)(2,1)S(1)} %get-tuple-element.13.refs_1_, ...), custom_call_target="tpu_custom_call" | custom-call | tf_op jit(solution)/shard_map/store/pallas_call | solution.py:510

commit v7 on v6

--- a/solution.py
+++ b/solution.py
@@ -48,7 +48,7 @@
     lens_v, assign_s, padded, qslot, gslot, kown, vown, kprev, vprev, qr, gr, qt, gt,
     ko, vo, kot, vot, kp, vp, kpt, vpt, bias, expo, dpo, pb, sb, oto, stat,
     part_p, part_o, sum_send, sum_near, far_send_buf, far_buf, own_send, own_near,
-    o_mine, o_near, q_mine, q_near,
+    o_mine, o_send, o_near, q_mine, q_send, q_near,
     loc_sem, far_ks, far_kr, far_vs, far_vr, rel_ks, rel_kr, rel_vs, rel_vr,
     near_s, near_r, p_s, p_r, f_s, f_r, o_s, o_r, oq_s, oq_r,
 ):
@@ -116,10 +116,10 @@
 
     @pl.when(has_next)
     def _():
-        for copy in far_k:
+        for copy in far_k + far_v:
             copy.start()
 
-    for copy in near:
+    for copy in near[:2]:
         copy.start()
 
     docs = lens_v.shape[0]
@@ -136,12 +136,6 @@
     upto = lax.broadcasted_iota(jnp.int32, (wide, wide), 1)
     lower = jnp.where(upto <= until, 1.0, 0.0).astype(BF16)
     sums = dot(lower, both, NT)
-
-    @pl.when(has_next)
-    def _():
-        for copy in far_v:
-            copy.start()
-
     base = chip * (GROUP * SPAN)
     ends = sums[:, 0:1] * 256.0 + sums[:, 1:2] - base.astype(F32)
     least = -base.astype(F32)
@@ -156,6 +150,9 @@
             if b == j:
                 ok = ok & (key_row <= query_col)
             bias[j, b * SPAN : (b + 1) * SPAN] = jnp.where(ok, 0.0, -1e30)
+
+    for copy in near[2:]:
+        copy.start()
 
     local[3].wait()
     back = jnp.maximum(chip - 1, 0)
@@ -320,9 +317,10 @@
         sum_send[a] = part_p[theirs_of(there, a)].astype(BF16)
         swap_p[a].start()
 
-    swap_out = remote(o_mine, o_near, oq_s.at[GROUP], oq_r.at[GROUP], beside)
-    swap_dq = [remote(q_mine.at[j], q_near.at[j], oq_s.at[j], oq_r.at[j], beside)
-               for j in range(GROUP)]
+    swap_out = remote(o_send, o_near, oq_s.at[0], oq_r.at[0], beside)
+    swap_dq = remote(q_send, q_near, oq_s.at[1], oq_r.at[1], beside)
+    for a in range(2):
+        o_send[a] = o_mine[theirs_of(here, a)]
     swap_out.start()
 
     def own_dscores(j):
@@ -332,7 +330,7 @@
             pb[j, rows] = pr.astype(BF16)
             sb[j, rows] = (pr * (dpo[j, rows] - deltas[j])).astype(BF16)
 
-    def own_grads(j):
+    def query_grads(j):
         own = slice(0, (j + 1) * SPAN)
         at = (j + 1) * SPAN
         dqt = dot(kot[:, own], sb[j, own], NN) + dot(kpt[:, j * SPAN :], sb[j, at:], NN)
@@ -340,14 +338,20 @@
         for h in range(heads):
             cols = slice(h * DIM, (h + 1) * DIM)
             q_mine[j, :, cols] = dqt[:, cols].T
+
+    def own_grads(j):
+        own = slice(0, (j + 1) * SPAN)
         part_o[0 : j + 1, :, 0:DIM] += spans(dot(sb[j, own], qr[j], NN) * ROOT)
         part_o[0 : j + 1, :, DIM:] += spans(dot(pb[j, own], gr[j], NN))
 
     own_dscores(0)
-    own_dscores(1)
-    own_grads(0)
-    own_dscores(2)
-    own_grads(1)
+    for j in range(1, GROUP):
+        own_dscores(j)
+        query_grads(j - 1)
+    query_grads(GROUP - 1)
+    for a in range(2):
+        q_send[a] = q_mine[theirs_of(here, a)]
+    swap_dq.start()
 
     for a in range(2):
         swap_p[a].wait_recv()
@@ -358,13 +362,8 @@
         def _(a=a):
             far_p[a].start()
 
-    for j in range(2):
-        swap_dq[j].start()
-    own_dscores(3)
-    own_grads(2)
-    swap_dq[2].start()
-    own_grads(3)
-    swap_dq[3].start()
+    for j in range(GROUP):
+        own_grads(j)
 
     swap_o = [remote(own_send.at[a], own_near.at[a], o_s.at[a], o_r.at[a], beside)
               for a in range(2)]
@@ -378,11 +377,10 @@
         dq[a, :, columns(core)] = q_mine[j]
     swap_out.wait_recv()
     for a in range(2):
-        attn[a, :, columns(other)] = o_near[mine_of(here, a)]
-    for j in range(GROUP):
-        swap_dq[j].wait_recv()
-    for a in range(2):
-        dq[a, :, columns(other)] = q_near[mine_of(here, a)]
+        attn[a, :, columns(other)] = o_near[a]
+    swap_dq.wait_recv()
+    for a in range(2):
+        dq[a, :, columns(other)] = q_near[a]
 
     @pl.when(jnp.logical_not(has_next))
     def _():
@@ -399,7 +397,7 @@
         dk[a] = total[:, 0:DIM].astype(BF16)
         dv[a] = total[:, DIM:].astype(BF16)
 
-    for copy in near + swap_p + [swap_out] + swap_dq + swap_o:
+    for copy in near + swap_p + [swap_out, swap_dq] + swap_o:
         copy.wait_send()
 
     @pl.when(has_next)
@@ -487,15 +485,17 @@
             pltpu.VMEM((2, SPAN, 2 * DIM), BF16),
             pltpu.VMEM((2, SPAN, 2 * DIM), BF16),
             pltpu.VMEM((GROUP, SPAN, half), BF16),
+            pltpu.VMEM((2, SPAN, half), BF16),
+            pltpu.VMEM((2, SPAN, half), BF16),
             pltpu.VMEM((GROUP, SPAN, half), BF16),
-            pltpu.VMEM((GROUP, SPAN, half), BF16),
-            pltpu.VMEM((GROUP, SPAN, half), BF16),
+            pltpu.VMEM((2, SPAN, half), BF16),
+            pltpu.VMEM((2, SPAN, half), BF16),
             dma((6,)),
             dma((2,)), dma((2,)), dma((2,)), dma((2,)),
             dma((2,)), dma((2,)), dma((2,)), dma((2,)),
             dma((4,)), dma((4,)),
             dma((2,)), dma((2,)), dma((2,)), dma((2,)), dma((2,)), dma((2,)),
-            dma((GROUP + 1,)), dma((GROUP + 1,)),
+            dma((2,)), dma((2,)),
         ],
         compiler_params=pltpu.CompilerParams(
             collective_id=0, has_side_effects=True, vmem_limit_bytes=40 * 2**20),

time: 27 us -> 26.8 us (level)
  no operation moved by 1% of the time
where the time goes in v7:
time: 26.8 us; the launch traced here: 26.7 us
  Pallas kernels  26 us (97%)
  between operations  0.64 us (2%)
    pallas_call x1, Pallas kernels, shards(): pl.pallas_call(functools.partial(main_kernel, count), out_shape=outs, in_...  25 us
    pallas_call x1, Pallas kernels, shards(): pl.pallas_call(store_kernel, out_shape=outs, in_specs=[pl.BlockSpec(memor...  1.07 us

profile of v7, /device:TPU:57, one launch (start us, length us, event | category | flops | bytes accessed | tf_op | source)
XLA Modules:
  0.0 26.7 jit_solution(16212054882975204530)
XLA Ops:
  0.6 25.0 %attend.1 = (bf16[2,128,1024]{2,1,0:T(8,128)(2,1)S(1)}, bf16[2,128,1024]{2,1,0:T(8,128)(2,1)S(1)}, bf16[2,128,128]{2,1,0:T(8,128)(2,1)S(1)}, bf16[2,128,128]{2,1,0:T(8,128)(2,1)S(1)}) custom-call(bf16[2,128,1024]{2,1,0:T(8,128)(2,1)} %bitcast.9, bf16[2,128,1024]{2,1,0:T(8,128)(2,1)} %bitcast.10, bf16[2,128,128]{2,1,0:T(8,128)(2,1)} %bitcast.11, ...), custom_call_target="tpu_custom_call" | custom-call | tf_op jit(solution)/shard_map/attend/pallas_call | solution.py:445
  25.6 1.1 %store.1 = (bf16[2,128,1024]{2,1,0:T(8,128)(2,1)}, bf16[2,128,1024]{2,1,0:T(8,128)(2,1)}, bf16[2,128,128]{2,1,0:T(8,128)(2,1)}, bf16[2,128,128]{2,1,0:T(8,128)(2,1)}) custom-call(bf16[2,128,1024]{2,1,0:T(8,128)(2,1)S(1)} %get-tuple-element.12.refs_0_, bf16[2,128,1024]{2,1,0:T(8,128)(2,1)S(1)} %get-tuple-element.13.refs_1_, ...), custom_call_target="tpu_custom_call" | custom-call | tf_op jit(solution)/shard_map/store/pallas_call | solution.py:510

commit v8 on v7

--- a/solution.py
+++ b/solution.py
@@ -50,7 +50,7 @@
     part_p, part_o, sum_send, sum_near, far_send_buf, far_buf, own_send, own_near,
     o_mine, o_send, o_near, q_mine, q_send, q_near,
     loc_sem, far_ks, far_kr, far_vs, far_vr, rel_ks, rel_kr, rel_vs, rel_vr,
-    near_s, near_r, p_s, p_r, f_s, f_r, o_s, o_r, oq_s, oq_r,
+    near_s, near_r, p_s, p_r, f_s, f_r, b_s, b_r, o_s, o_r, oq_s, oq_r,
 ):
     me = lax.axis_index("seq")
     grp = lax.axis_index("grp")
@@ -294,34 +294,49 @@
         part_p[j:, :, 0:DIM] += spans(dot(sb[j, at:], qr[j], NN) * ROOT)
         part_p[j:, :, DIM:] += spans(dot(pb[j, at:], gr[j], NN))
 
-    finish_out(0)
-    dp = prev_dprobs(0)
-    for j in range(1, GROUP):
-        finish_out(j)
-        next_dp = prev_dprobs(j)
-        prev_grads(j - 1, dp)
-        dp = next_dp
-    prev_grads(GROUP - 1, dp)
-
     def mine_of(spans, a):
         return jnp.where(core == 0, spans[a], spans[2 + a])
 
     def theirs_of(spans, a):
         return jnp.where(core == 0, spans[2 + a], spans[a])
 
-    swap_p = [remote(sum_send.at[a], sum_near.at[a], p_s.at[a], p_r.at[a], beside)
-              for a in range(2)]
-    far_p = [remote(far_send_buf.at[a], far_buf.at[a], f_s.at[a], f_r.at[a], before)
-             for a in range(2)]
-    for a in range(2):
-        sum_send[a] = part_p[theirs_of(there, a)].astype(BF16)
-        swap_p[a].start()
-
     swap_out = remote(o_send, o_near, oq_s.at[0], oq_r.at[0], beside)
     swap_dq = remote(q_send, q_near, oq_s.at[1], oq_r.at[1], beside)
+    swap_p = [remote(sum_send.at[r], sum_near.at[r], p_s.at[r], p_r.at[r], beside)
+              for r in range(2)]
+    far_p = [remote(far_send_buf.at[r], far_buf.at[2 * r + core], f_s.at[r], f_r.at[r], before)
+             for r in range(2)]
+    relay_p = [remote(far_buf.at[2 * r + core], far_buf.at[2 * r + core], b_s.at[r], b_r.at[r],
+                      beside) for r in range(2)]
+
+    def swap_round(r):
+        sum_send[r] = part_p[2 * r + other].astype(BF16)
+        swap_p[r].start()
+
+    def far_round(r):
+        swap_p[r].wait_recv()
+        far_send_buf[r] = (part_p[2 * r + core] + sum_near[r].astype(F32)).astype(BF16)
+
+        @pl.when(has_prev)
+        def _():
+            far_p[r].start()
+
+    for j in range(GROUP):
+        finish_out(j)
     for a in range(2):
         o_send[a] = o_mine[theirs_of(here, a)]
     swap_out.start()
+
+    dp = prev_dprobs(0)
+    for j in range(GROUP):
+        next_dp = prev_dprobs(j + 1) if j < GROUP - 1 else None
+        prev_grads(j, dp)
+        dp = next_dp
+        if j == 1:
+            swap_round(0)
+        if j == 2:
+            far_round(0)
+    swap_round(1)
 
     def own_dscores(j):
         for at in range(0, (j + 1) * SPAN, PIECE):
@@ -345,22 +360,23 @@
         part_o[0 : j + 1, :, DIM:] += spans(dot(pb[j, own], gr[j], NN))
 
     own_dscores(0)
-    for j in range(1, GROUP):
-        own_dscores(j)
-        query_grads(j - 1)
-    query_grads(GROUP - 1)
+    own_dscores(1)
+    query_grads(0)
+    far_round(1)
+    own_dscores(2)
+    query_grads(1)
+    own_dscores(3)
+    query_grads(2)
+    query_grads(3)
     for a in range(2):
         q_send[a] = q_mine[theirs_of(here, a)]
     swap_dq.start()
 
-    for a in range(2):
-        swap_p[a].wait_recv()
-        far_send_buf[a] = (
-            part_p[mine_of(there, a)] + sum_near[a].astype(F32)).astype(BF16)
-
-        @pl.when(has_prev)
-        def _(a=a):
-            far_p[a].start()
+    @pl.when(has_next)
+    def _():
+        for r in range(2):
+            far_p[r].wait_recv()
+            relay_p[r].start()
 
     for j in range(GROUP):
         own_grads(j)
@@ -386,14 +402,15 @@
     def _():
         far_buf[...] = jnp.zeros_like(far_buf)
 
+    @pl.when(has_next)
+    def _():
+        for r in range(2):
+            relay_p[r].wait_recv()
+
     for a in range(2):
         swap_o[a].wait_recv()
-
-        @pl.when(has_next)
-        def _(a=a):
-            far_p[a].wait_recv()
-
-        total = part_o[mine_of(here, a)] + own_near[a].astype(F32) + far_buf[a].astype(F32)
+        span = mine_of(here, a)
+        total = part_o[span] + own_near[a].astype(F32) + far_buf[span].astype(F32)
         dk[a] = total[:, 0:DIM].astype(BF16)
         dv[a] = total[:, DIM:].astype(BF16)
 
@@ -402,7 +419,7 @@
 
     @pl.when(has_next)
     def _():
-        for copy in far_k + far_v:
+        for copy in far_k + far_v + relay_p:
             copy.wait_send()
 
     @pl.when(has_prev)
@@ -481,7 +498,7 @@
             pltpu.VMEM((2, SPAN, 2 * DIM), BF16),
             pltpu.VMEM((2, SPAN, 2 * DIM), BF16),
             pltpu.VMEM((2, SPAN, 2 * DIM), BF16),
-            pltpu.VMEM((2, SPAN, 2 * DIM), BF16),
+            pltpu.VMEM((GROUP, SPAN, 2 * DIM), BF16),
             pltpu.VMEM((2, SPAN, 2 * DIM), BF16),
             pltpu.VMEM((2, SPAN, 2 * DIM), BF16),
             pltpu.VMEM((GROUP, SPAN, half), BF16),
@@ -495,7 +512,7 @@
             dma((2,)), dma((2,)), dma((2,)), dma((2,)),
             dma((4,)), dma((4,)),
             dma((2,)), dma((2,)), dma((2,)), dma((2,)), dma((2,)), dma((2,)),
-            dma((2,)), dma((2,)),
+            dma((2,)), dma((2,)), dma((2,)), dma((2,)),
         ],
         compiler_params=pltpu.CompilerParams(
             collective_id=0, has_side_effects=True, vmem_limit_bytes=40 * 2**20),

time: 26.8 us -> 29 us (1.082)
  Pallas kernels: 26 us -> 28.2 us
    pallas_call x1, Pallas kernels: 25 us -> 27.2 us  [shards(): pl.pallas_call(functools.partial(main_kernel, count), out_shape=outs, in_...]
where the time goes in v8:
time: 29 us; the launch traced here: 28.9 us
  Pallas kernels  28.2 us (97%)
  between operations  0.64 us (2%)
    pallas_call x1, Pallas kernels, shards(): pl.pallas_call(functools.partial(main_kernel, count), out_shape=outs, in_...  27.2 us
    pallas_call x1, Pallas kernels, shards(): pl.pallas_call(store_kernel, out_shape=outs, in_specs=[pl.BlockSpec(memor...  1.07 us

profile of v8, /device:TPU:57, one launch (start us, length us, event | category | flops | bytes accessed | tf_op | source)
XLA Modules:
  0.0 28.9 jit_solution(248648505676037572)
XLA Ops:
  0.6 27.2 %attend.1 = (bf16[2,128,1024]{2,1,0:T(8,128)(2,1)S(1)}, bf16[2,128,1024]{2,1,0:T(8,128)(2,1)S(1)}, bf16[2,128,128]{2,1,0:T(8,128)(2,1)S(1)}, bf16[2,128,128]{2,1,0:T(8,128)(2,1)S(1)}) custom-call(bf16[2,128,1024]{2,1,0:T(8,128)(2,1)} %bitcast.9, bf16[2,128,1024]{2,1,0:T(8,128)(2,1)} %bitcast.10, bf16[2,128,128]{2,1,0:T(8,128)(2,1)} %bitcast.11, ...), custom_call_target="tpu_custom_call" | custom-call | tf_op jit(solution)/shard_map/attend/pallas_call | solution.py:462
  27.8 1.1 %store.1 = (bf16[2,128,1024]{2,1,0:T(8,128)(2,1)}, bf16[2,128,1024]{2,1,0:T(8,128)(2,1)}, bf16[2,128,128]{2,1,0:T(8,128)(2,1)}, bf16[2,128,128]{2,1,0:T(8,128)(2,1)}) custom-call(bf16[2,128,1024]{2,1,0:T(8,128)(2,1)S(1)} %get-tuple-element.12.refs_0_, bf16[2,128,1024]{2,1,0:T(8,128)(2,1)S(1)} %get-tuple-element.13.refs_1_, ...), custom_call_target="tpu_custom_call" | custom-call | tf_op jit(solution)/shard_map/store/pallas_call | solution.py:527

commit v9 on v7

--- a/solution.py
+++ b/solution.py
@@ -16,6 +16,7 @@
 BF16 = jnp.bfloat16
 NT = (((1,), (1,)), ((), ()))
 NN = (((1,), (0,)), ((), ()))
+TN = (((0,), (0,)), ((), ()))
 ROOT = 1.0 / math.sqrt(DIM)
 PIECE = 32
 
@@ -333,11 +334,11 @@
     def query_grads(j):
         own = slice(0, (j + 1) * SPAN)
         at = (j + 1) * SPAN
-        dqt = dot(kot[:, own], sb[j, own], NN) + dot(kpt[:, j * SPAN :], sb[j, at:], NN)
-        dqt = (dqt * ROOT).astype(BF16)
+        grad = dot(sb[j, own], ko[own], TN) + dot(sb[j, at:], kp[j * SPAN :], TN)
+        grad = (grad * ROOT).astype(BF16)
         for h in range(heads):
             cols = slice(h * DIM, (h + 1) * DIM)
-            q_mine[j, :, cols] = dqt[:, cols].T
+            q_mine[j, :, cols] = grad[cols]
 
     def own_grads(j):
         own = slice(0, (j + 1) * SPAN)

time: 26.8 us -> 26.8 us (level)
  no operation moved by 1% of the time
where the time goes in v9:
time: 26.8 us; the launch traced here: 26.5 us
  Pallas kernels  25.9 us (97%)
  between operations  0.64 us (2%)
    pallas_call x1, Pallas kernels, shards(): pl.pallas_call(functools.partial(main_kernel, count), out_shape=outs, in_...  24.8 us
    pallas_call x1, Pallas kernels, shards(): pl.pallas_call(store_kernel, out_shape=outs, in_specs=[pl.BlockSpec(memor...  1.07 us

profile of v9, /device:TPU:57, one launch (start us, length us, event | category | flops | bytes accessed | tf_op | source)
XLA Modules:
  0.0 26.5 jit_solution(11730559243140629607)
XLA Ops:
  0.6 24.8 %attend.1 = (bf16[2,128,1024]{2,1,0:T(8,128)(2,1)S(1)}, bf16[2,128,1024]{2,1,0:T(8,128)(2,1)S(1)}, bf16[2,128,128]{2,1,0:T(8,128)(2,1)S(1)}, bf16[2,128,128]{2,1,0:T(8,128)(2,1)S(1)}) custom-call(bf16[2,128,1024]{2,1,0:T(8,128)(2,1)} %bitcast.9, bf16[2,128,1024]{2,1,0:T(8,128)(2,1)} %bitcast.10, bf16[2,128,128]{2,1,0:T(8,128)(2,1)} %bitcast.11, ...), custom_call_target="tpu_custom_call" | custom-call | tf_op jit(solution)/shard_map/attend/pallas_call | solution.py:446
  25.4 1.1 %store.1 = (bf16[2,128,1024]{2,1,0:T(8,128)(2,1)}, bf16[2,128,1024]{2,1,0:T(8,128)(2,1)}, bf16[2,128,128]{2,1,0:T(8,128)(2,1)}, bf16[2,128,128]{2,1,0:T(8,128)(2,1)}) custom-call(bf16[2,128,1024]{2,1,0:T(8,128)(2,1)S(1)} %get-tuple-element.12.refs_0_, bf16[2,128,1024]{2,1,0:T(8,128)(2,1)S(1)} %get-tuple-element.13.refs_1_, ...), custom_call_target="tpu_custom_call" | custom-call | tf_op jit(solution)/shard_map/store/pallas_call | solution.py:511

commit v10 on v9

--- a/solution.py
+++ b/solution.py
@@ -51,7 +51,7 @@
     part_p, part_o, sum_send, sum_near, far_send_buf, far_buf, own_send, own_near,
     o_mine, o_send, o_near, q_mine, q_send, q_near,
     loc_sem, far_ks, far_kr, far_vs, far_vr, rel_ks, rel_kr, rel_vs, rel_vr,
-    near_s, near_r, p_s, p_r, f_s, f_r, o_s, o_r, oq_s, oq_r,
+    near_s, near_r, p_s, p_r, f_s, f_r, b_s, b_r, o_s, o_r, oq_s, oq_r,
 ):
     me = lax.axis_index("seq")
     grp = lax.axis_index("grp")
@@ -195,15 +195,20 @@
             top = fold(piece, jnp.max) if top is None else jnp.maximum(top, fold(piece, jnp.max))
         return jnp.max(top, axis=0, keepdims=True)
 
-    def exponentials(j, first, n, top, low=None):
-        total = None
+    def exponentials(j, first, n, top):
+        total = jnp.zeros((8, width), F32)
         for at in range(0, n, PIECE):
             rows = slice(first + at, first + at + PIECE)
             e = jnp.exp2(expo[j, rows] - top)
             expo[j, rows] = e
-            if low is not None:
-                low[j, rows] = e.astype(BF16)
-            total = fold(e, jnp.sum) if total is None else total + fold(e, jnp.sum)
+            total = total + fold(e, jnp.sum)
+        return jnp.sum(total, axis=0, keepdims=True)
+
+    def weighted(j, first, dp):
+        total = jnp.zeros((8, width), F32)
+        for at in range(0, dp.shape[0], PIECE):
+            rows = slice(first + at, first + at + PIECE)
+            total = total + fold(expo[j, rows] * dp[at : at + PIECE], jnp.sum)
         return jnp.sum(total, axis=0, keepdims=True)
 
     tops = []
@@ -214,8 +219,9 @@
     for j in range(GROUP):
         n = (j + 1) * SPAN
         stat[j, 0:1] = tops[j]
-        stat[j, 1:2] = exponentials(j, 0, n, tops[j], pb)
-        oto[j] = dot(vot[:, 0:n], pb[j, 0:n], NN)
+        stat[j, 1:2] = exponentials(j, 0, n, tops[j])
+        stat[j, 2:3] = weighted(j, 0, dpo[j, 0:n])
+        oto[j] = dot(vot[:, 0:n], expo[j, 0:n].astype(BF16), NN)
 
     @pl.when(has_prev)
     def _():
@@ -256,13 +262,6 @@
                     far_v[a].wait_recv()
                     relay_v[a].start()
 
-    for j in range(GROUP):
-        for at in range((j + 1) * SPAN, expo.shape[1], PIECE):
-            rows = slice(at, at + PIECE)
-            pr = expo[j, rows] * norms[j]
-            expo[j, rows] = pr
-            pb[j, rows] = pr.astype(BF16)
-
     @pl.when(has_prev)
     def _():
         for a in range(2):
@@ -274,55 +273,75 @@
         vp[rows] = vb
         vpt[:, rows] = vb.T
 
+    def mine_of(spans, a):
+        return jnp.where(core == 0, spans[a], spans[2 + a])
+
+    def theirs_of(spans, a):
+        return jnp.where(core == 0, spans[2 + a], spans[a])
+
+    my_pair = pl.ds(2 * core, 2)
+    swap_p = remote(sum_send, sum_near, p_s.at[0], p_r.at[0], beside)
+    far_p = remote(far_send_buf, far_buf.at[my_pair], f_s.at[0], f_r.at[0], before)
+    relay_p = remote(far_buf.at[my_pair], far_buf.at[my_pair], b_s.at[0], b_r.at[0], beside)
+
+    def give(pair):
+        sum_send[...] = part_p[2 * pair : 2 * pair + 2].astype(BF16)
+        swap_p.start()
+
+    def send_back(pair):
+        swap_p.wait_recv()
+        for i in range(2):
+            far_send_buf[i] = (part_p[2 * pair + i] + sum_near[i].astype(F32)).astype(BF16)
+
+        @pl.when(has_prev)
+        def _():
+            far_p.start()
+
     deltas = []
 
-    def finish_out(j):
+    def prev_grads(j, dp):
+        at = (j + 1) * SPAN
+        delta = alphas[j] * stat[j, 2:3] + norms[j] * weighted(j, at, dp)
+        deltas.append(delta)
+        for p in range(0, dp.shape[0], PIECE):
+            rows = slice(at + p, at + p + PIECE)
+            pr = expo[j, rows] * norms[j]
+            pb[j, rows] = pr.astype(BF16)
+            sb[j, rows] = (pr * (dp[p : p + PIECE] - delta)).astype(BF16)
+        part_p[j:, :, 0:DIM] += spans(dot(sb[j, at:], qr[j], NN) * ROOT)
+        part_p[j:, :, DIM:] += spans(dot(pb[j, at:], gr[j], NN))
+
+    dp = dot(vp[...], gt[0], NN)
+    for j in range(GROUP):
+        next_dp = dot(vp[(j + 1) * SPAN :], gt[j + 1], NN) if j < GROUP - 1 else None
+        prev_grads(j, dp)
+        dp = next_dp
+        if j == 1:
+
+            @pl.when(core == 1)
+            def _():
+                give(0)
+
+    @pl.when(core == 0)
+    def _():
+        give(1)
+        send_back(0)
+
+    swap_out = remote(o_send, o_near, oq_s.at[0], oq_r.at[0], beside)
+    swap_dq = remote(q_send, q_near, oq_s.at[1], oq_r.at[1], beside)
+    for j in range(GROUP):
         out = oto[j] * alphas[j] + dot(vpt[:, j * SPAN :], pb[j, (j + 1) * SPAN :], NN)
-        deltas.append(jnp.sum(out * gt[j].astype(F32), axis=0, keepdims=True))
         out = out.astype(BF16)
         for h in range(heads):
             cols = slice(h * DIM, (h + 1) * DIM)
             o_mine[j, :, cols] = out[:, cols].T
-
-    def prev_dprobs(j):
-        return dot(vp[j * SPAN :], gt[j], NN)
-
-    def prev_grads(j, dp):
-        at = (j + 1) * SPAN
-        for p in range(0, dp.shape[0], PIECE):
-            rows = slice(at + p, at + p + PIECE)
-            sb[j, rows] = (expo[j, rows] * (dp[p : p + PIECE] - deltas[j])).astype(BF16)
-        part_p[j:, :, 0:DIM] += spans(dot(sb[j, at:], qr[j], NN) * ROOT)
-        part_p[j:, :, DIM:] += spans(dot(pb[j, at:], gr[j], NN))
-
-    finish_out(0)
-    dp = prev_dprobs(0)
-    for j in range(1, GROUP):
-        finish_out(j)
-        next_dp = prev_dprobs(j)
-        prev_grads(j - 1, dp)
-        dp = next_dp
-    prev_grads(GROUP - 1, dp)
-
-    def mine_of(spans, a):
-        return jnp.where(core == 0, spans[a], spans[2 + a])
-
-    def theirs_of(spans, a):
-        return jnp.where(core == 0, spans[2 + a], spans[a])
-
-    swap_p = [remote(sum_send.at[a], sum_near.at[a], p_s.at[a], p_r.at[a], beside)
-              for a in range(2)]
-    far_p = [remote(far_send_buf.at[a], far_buf.at[a], f_s.at[a], f_r.at[a], before)
-             for a in range(2)]
-    for a in range(2):
-        sum_send[a] = part_p[theirs_of(there, a)].astype(BF16)
-        swap_p[a].start()
-
-    swap_out = remote(o_send, o_near, oq_s.at[0], oq_r.at[0], beside)
-    swap_dq = remote(q_send, q_near, oq_s.at[1], oq_r.at[1], beside)
     for a in range(2):
         o_send[a] = o_mine[theirs_of(here, a)]
     swap_out.start()
+
+    @pl.when(core == 1)
+    def _():
+        send_back(1)
 
     def own_dscores(j):
         for at in range(0, (j + 1) * SPAN, PIECE):
@@ -354,14 +373,10 @@
         q_send[a] = q_mine[theirs_of(here, a)]
     swap_dq.start()
 
-    for a in range(2):
-        swap_p[a].wait_recv()
-        far_send_buf[a] = (
-            part_p[mine_of(there, a)] + sum_near[a].astype(F32)).astype(BF16)
-
-        @pl.when(has_prev)
-        def _(a=a):
-            far_p[a].start()
+    @pl.when(has_next)
+    def _():
+        far_p.wait_recv()
+        relay_p.start()
 
     for j in range(GROUP):
         own_grads(j)
@@ -387,28 +402,28 @@
     def _():
         far_buf[...] = jnp.zeros_like(far_buf)
 
+    @pl.when(has_next)
+    def _():
+        relay_p.wait_recv()
+
     for a in range(2):
         swap_o[a].wait_recv()
-
-        @pl.when(has_next)
-        def _(a=a):
-            far_p[a].wait_recv()
-
-        total = part_o[mine_of(here, a)] + own_near[a].astype(F32) + far_buf[a].astype(F32)
+        span = mine_of(here, a)
+        total = part_o[span] + own_near[a].astype(F32) + far_buf[span].astype(F32)
         dk[a] = total[:, 0:DIM].astype(BF16)
         dv[a] = total[:, DIM:].astype(BF16)
 
-    for copy in near + swap_p + [swap_out, swap_dq] + swap_o:
+    for copy in near + [swap_p, swap_out, swap_dq] + swap_o:
         copy.wait_send()
 
     @pl.when(has_next)
     def _():
-        for copy in far_k + far_v:
+        for copy in far_k + far_v + [relay_p]:
             copy.wait_send()
 
     @pl.when(has_prev)
     def _():
-        for copy in relay_k + relay_v + far_p:
+        for copy in relay_k + relay_v + [far_p]:
             copy.wait_send()
 
 
@@ -482,7 +497,7 @@
             pltpu.VMEM((2, SPAN, 2 * DIM), BF16),
             pltpu.VMEM((2, SPAN, 2 * DIM), BF16),
             pltpu.VMEM((2, SPAN, 2 * DIM), BF16),
-            pltpu.VMEM((2, SPAN, 2 * DIM), BF16),
+            pltpu.VMEM((GROUP, SPAN, 2 * DIM), BF16),
             pltpu.VMEM((2, SPAN, 2 * DIM), BF16),
             pltpu.VMEM((2, SPAN, 2 * DIM), BF16),
             pltpu.VMEM((GROUP, SPAN, half), BF16),
@@ -495,8 +510,8 @@
             dma((2,)), dma((2,)), dma((2,)), dma((2,)),
             dma((2,)), dma((2,)), dma((2,)), dma((2,)),
             dma((4,)), dma((4,)),
-            dma((2,)), dma((2,)), dma((2,)), dma((2,)), dma((2,)), dma((2,)),
-            dma((2,)), dma((2,)),
+            dma((1,)), dma((1,)), dma((1,)), dma((1,)), dma((1,)), dma((1,)),
+            dma((2,)), dma((2,)), dma((2,)), dma((2,)),
         ],
         compiler_params=pltpu.CompilerParams(
             collective_id=0, has_side_effects=True, vmem_limit_bytes=40 * 2**20),

time: 26.8 us -> 28.2 us (1.052)
  Pallas kernels: 25.9 us -> 27.5 us
    pallas_call x1, Pallas kernels: 24.8 us -> 26.4 us  [shards(): pl.pallas_call(functools.partial(main_kernel, count), out_shape=outs, in_...]
where the time goes in v10:
time: 28.2 us; the launch traced here: 28.1 us
  Pallas kernels  27.5 us (98%)
  between operations  0.64 us (2%)
    pallas_call x1, Pallas kernels, shards(): pl.pallas_call(functools.partial(main_kernel, count), out_shape=outs, in_...  26.4 us
    pallas_call x1, Pallas kernels, shards(): pl.pallas_call(store_kernel, out_shape=outs, in_specs=[pl.BlockSpec(memor...  1.07 us

profile of v10, /device:TPU:57, one launch (start us, length us, event | category | flops | bytes accessed | tf_op | source)
XLA Modules:
  0.0 28.1 jit_solution(16010170764702410314)
XLA Ops:
  0.6 26.4 %attend.1 = (bf16[2,128,1024]{2,1,0:T(8,128)(2,1)S(1)}, bf16[2,128,1024]{2,1,0:T(8,128)(2,1)S(1)}, bf16[2,128,128]{2,1,0:T(8,128)(2,1)S(1)}, bf16[2,128,128]{2,1,0:T(8,128)(2,1)S(1)}) custom-call(bf16[2,128,1024]{2,1,0:T(8,128)(2,1)} %bitcast.9, bf16[2,128,1024]{2,1,0:T(8,128)(2,1)} %bitcast.10, bf16[2,128,128]{2,1,0:T(8,128)(2,1)} %bitcast.11, ...), custom_call_target="tpu_custom_call" | custom-call | tf_op jit(solution)/shard_map/attend/pallas_call | solution.py:461
  27.0 1.1 %store.1 = (bf16[2,128,1024]{2,1,0:T(8,128)(2,1)}, bf16[2,128,1024]{2,1,0:T(8,128)(2,1)}, bf16[2,128,128]{2,1,0:T(8,128)(2,1)}, bf16[2,128,128]{2,1,0:T(8,128)(2,1)}) custom-call(bf16[2,128,1024]{2,1,0:T(8,128)(2,1)S(1)} %get-tuple-element.12.refs_0_, bf16[2,128,1024]{2,1,0:T(8,128)(2,1)S(1)} %get-tuple-element.13.refs_1_, ...), custom_call_target="tpu_custom_call" | custom-call | tf_op jit(solution)/shard_map/store/pallas_call | solution.py:526

commit v11 on v9

--- a/solution.py
+++ b/solution.py
@@ -18,6 +18,8 @@
 NN = (((1,), (0,)), ((), ()))
 TN = (((0,), (0,)), ((), ()))
 ROOT = 1.0 / math.sqrt(DIM)
+FAR = 64
+BACK = 32
 PIECE = 32
 
 
@@ -84,14 +86,21 @@
         pltpu.make_async_copy(q.at[:, :, columns(core)], qslot.at[own_slots], loc_sem.at[4]),
         pltpu.make_async_copy(g.at[:, :, columns(core)], gslot.at[own_slots], loc_sem.at[5]),
     ]
-    far_k = [remote(k.at[a], kprev.at[2 * core + a], far_ks.at[a], far_kr.at[a], after)
-             for a in range(2)]
-    far_v = [remote(v.at[a], vprev.at[2 * core + a], far_vs.at[a], far_vr.at[a], after)
-             for a in range(2)]
-    relay_k = [remote(kprev.at[2 * core + a], kprev.at[2 * core + a], rel_ks.at[a], rel_kr.at[a],
-                      beside) for a in range(2)]
-    relay_v = [remote(vprev.at[2 * core + a], vprev.at[2 * core + a], rel_vs.at[a], rel_vr.at[a],
-                      beside) for a in range(2)]
+    def pieces(ref, span):
+        return [ref.at[span, pl.ds(at, FAR)] for at in range(0, SPAN, FAR)]
+
+    def far_copies(src, dst, send, recv):
+        ends = [(x, y) for a in range(2) for x, y in zip(pieces(src, a), pieces(dst, 2 * core + a))]
+        return [remote(x, y, send.at[i], recv.at[i], after) for i, (x, y) in enumerate(ends)]
+
+    def relay_copies(dst, send, recv):
+        ends = [x for a in range(2) for x in pieces(dst, 2 * core + a)]
+        return [remote(x, x, send.at[i], recv.at[i], beside) for i, x in enumerate(ends)]
+
+    far_k = far_copies(k, kprev, far_ks, far_kr)
+    far_v = far_copies(v, vprev, far_vs, far_vr)
+    relay_k = relay_copies(kprev, rel_ks, rel_kr)
+    relay_v = relay_copies(vprev, rel_vs, rel_vr)
     near = [
         remote(k, kown.at[own_slots], near_s.at[0], near_r.at[0], beside),
         remote(v, vown.at[own_slots], near_s.at[1], near_r.at[1], beside),
@@ -219,11 +228,11 @@
 
     @pl.when(has_prev)
     def _():
-        for a in range(2):
-            far_k[a].wait_recv()
-            relay_k[a].start()
-        for a in range(2):
-            relay_k[a].wait_recv()
+        for far, relay in zip(far_k, relay_k):
+            far.wait_recv()
+            relay.start()
+        for relay in relay_k:
+            relay.wait_recv()
 
     @pl.when(jnp.logical_not(has_prev))
     def _():
@@ -252,9 +261,9 @@
 
             @pl.when(has_prev)
             def _():
-                for a in range(2):
-                    far_v[a].wait_recv()
-                    relay_v[a].start()
+                for far, relay in zip(far_v, relay_v):
+                    far.wait_recv()
+                    relay.start()
 
     for j in range(GROUP):
         for at in range((j + 1) * SPAN, expo.shape[1], PIECE):
@@ -265,8 +274,8 @@
 
     @pl.when(has_prev)
     def _():
-        for a in range(2):
-            relay_v[a].wait_recv()
+        for relay in relay_v:
+            relay.wait_recv()
 
     for i in range(GROUP):
         rows = slice(i * SPAN, (i + 1) * SPAN)
@@ -312,8 +321,11 @@
 
     swap_p = [remote(sum_send.at[a], sum_near.at[a], p_s.at[a], p_r.at[a], beside)
               for a in range(2)]
-    far_p = [remote(far_send_buf.at[a], far_buf.at[a], f_s.at[a], f_r.at[a], before)
-             for a in range(2)]
+    far_p = [
+        remote(far_send_buf.at[a, pl.ds(at, BACK)], far_buf.at[a, pl.ds(at, BACK)],
+               f_s.at[a, at // BACK], f_r.at[a, at // BACK], before)
+        for a in range(2) for at in range(0, SPAN, BACK)
+    ]
     for a in range(2):
         sum_send[a] = part_p[theirs_of(there, a)].astype(BF16)
         swap_p[a].start()
@@ -361,7 +373,8 @@
 
         @pl.when(has_prev)
         def _(a=a):
-            far_p[a].start()
+            for copy in far_p[a * (SPAN // BACK) : (a + 1) * (SPAN // BACK)]:
+                copy.start()
 
     for j in range(GROUP):
         own_grads(j)
@@ -392,7 +405,8 @@
 
         @pl.when(has_next)
         def _(a=a):
-            far_p[a].wait_recv()
+            for copy in far_p[a * (SPAN // BACK) : (a + 1) * (SPAN // BACK)]:
+                copy.wait_recv()
 
         total = part_o[mine_of(here, a)] + own_near[a].astype(F32) + far_buf[a].astype(F32)
         dk[a] = total[:, 0:DIM].astype(BF16)
@@ -437,6 +451,7 @@
     shape = jax.ShapeDtypeStruct
     keyed = GROUP * SPAN
     seen = keyed + SPAN
+    moves = 2 * SPAN // FAR
     outs = (
         shape((2, SPAN, width), BF16),
         shape((2, SPAN, width), BF16),
@@ -492,10 +507,11 @@
             pltpu.VMEM((2, SPAN, half), BF16),
             pltpu.VMEM((2, SPAN, half), BF16),
             dma((6,)),
-            dma((2,)), dma((2,)), dma((2,)), dma((2,)),
-            dma((2,)), dma((2,)), dma((2,)), dma((2,)),
+            dma((moves,)), dma((moves,)), dma((moves,)), dma((moves,)),
+            dma((moves,)), dma((moves,)), dma((moves,)), dma((moves,)),
             dma((4,)), dma((4,)),
-            dma((2,)), dma((2,)), dma((2,)), dma((2,)), dma((2,)), dma((2,)),
+            dma((2,)), dma((2,)), dma((2, SPAN // BACK)), dma((2, SPAN // BACK)),
+            dma((2,)), dma((2,)),
             dma((2,)), dma((2,)),
         ],
         compiler_params=pltpu.CompilerParams(

time: 26.8 us -> 27 us (level)
  no operation moved by 1% of the time
where the time goes in v11:
time: 27 us; the launch traced here: 26.8 us
  Pallas kernels  26.1 us (97%)
  between operations  0.64 us (2%)
    pallas_call x1, Pallas kernels, shards(): pl.pallas_call(functools.partial(main_kernel, count), out_shape=outs, in_...  25.1 us
    pallas_call x1, Pallas kernels, shards(): pl.pallas_call(store_kernel, out_shape=outs, in_specs=[pl.BlockSpec(memor...  1.07 us

profile of v11, /device:TPU:57, one launch (start us, length us, event | category | flops | bytes accessed | tf_op | source)
XLA Modules:
  0.0 26.8 jit_solution(9326844513740602041)
XLA Ops:
  0.6 25.1 %attend.1 = (bf16[2,128,1024]{2,1,0:T(8,128)(2,1)S(1)}, bf16[2,128,1024]{2,1,0:T(8,128)(2,1)S(1)}, bf16[2,128,128]{2,1,0:T(8,128)(2,1)S(1)}, bf16[2,128,128]{2,1,0:T(8,128)(2,1)S(1)}) custom-call(bf16[2,128,1024]{2,1,0:T(8,128)(2,1)} %bitcast.9, bf16[2,128,1024]{2,1,0:T(8,128)(2,1)} %bitcast.10, bf16[2,128,128]{2,1,0:T(8,128)(2,1)} %bitcast.11, ...), custom_call_target="tpu_custom_call" | custom-call | tf_op jit(solution)/shard_map/attend/pallas_call | solution.py:461
  25.7 1.1 %store.1 = (bf16[2,128,1024]{2,1,0:T(8,128)(2,1)}, bf16[2,128,1024]{2,1,0:T(8,128)(2,1)}, bf16[2,128,128]{2,1,0:T(8,128)(2,1)}, bf16[2,128,128]{2,1,0:T(8,128)(2,1)}) custom-call(bf16[2,128,1024]{2,1,0:T(8,128)(2,1)S(1)} %get-tuple-element.12.refs_0_, bf16[2,128,1024]{2,1,0:T(8,128)(2,1)S(1)} %get-tuple-element.13.refs_1_, ...), custom_call_target="tpu_custom_call" | custom-call | tf_op jit(solution)/shard_map/store/pallas_call | solution.py:527

commit v12 on v9

--- a/solution.py
+++ b/solution.py
@@ -50,7 +50,7 @@
     ko, vo, kot, vot, kp, vp, kpt, vpt, bias, expo, dpo, pb, sb, oto, stat,
     part_p, part_o, sum_send, sum_near, far_send_buf, far_buf, own_send, own_near,
     o_mine, o_send, o_near, q_mine, q_send, q_near,
-    loc_sem, far_ks, far_kr, far_vs, far_vr, rel_ks, rel_kr, rel_vs, rel_vr,
+    arrived, loc_sem, far_ks, far_kr, far_vs, far_vr, rel_ks, rel_kr, rel_vs, rel_vr,
     near_s, near_r, p_s, p_r, f_s, f_r, o_s, o_r, oq_s, oq_r,
 ):
     me = lax.axis_index("seq")
@@ -106,17 +106,13 @@
     def _():
         pl.semaphore_signal(barrier, inc=1, device_id=(before, grp), device_id_type=MESH)
 
-    @pl.when(has_next)
-    def _():
-        pl.semaphore_signal(barrier, inc=1, device_id=(after, grp), device_id_type=MESH)
-
     for copy in local:
         copy.start()
-    pl.semaphore_wait(
-        barrier, 1 + has_prev.astype(jnp.int32) + has_next.astype(jnp.int32))
+    pl.semaphore_wait(barrier, 1 + has_next.astype(jnp.int32))
 
     @pl.when(has_next)
     def _():
+        pl.semaphore_signal(arrived, inc=1, device_id=(after, grp), device_id_type=MESH)
         for copy in far_k + far_v:
             copy.start()
 
@@ -219,6 +215,7 @@
 
     @pl.when(has_prev)
     def _():
+        pl.semaphore_wait(arrived, 1)
         for a in range(2):
             far_k[a].wait_recv()
             relay_k[a].start()
@@ -491,6 +488,7 @@
             pltpu.VMEM((GROUP, SPAN, half), BF16),
             pltpu.VMEM((2, SPAN, half), BF16),
             pltpu.VMEM((2, SPAN, half), BF16),
+            pltpu.SemaphoreType.REGULAR,
             dma((6,)),
             dma((2,)), dma((2,)), dma((2,)), dma((2,)),
             dma((2,)), dma((2,)), dma((2,)), dma((2,)),

time: 26.8 us -> 24.8 us (0.925)
  Pallas kernels: 25.9 us -> 23.9 us
    pallas_call x1, Pallas kernels: 24.8 us -> 22.8 us  [shards(): pl.pallas_call(functools.partial(main_kernel, count), out_shape=outs, in_...]
where the time goes in v12:
time: 24.8 us; the launch traced here: 24.5 us
  Pallas kernels  23.9 us (96%)
  between operations  0.64 us (3%)
    pallas_call x1, Pallas kernels, shards(): pl.pallas_call(functools.partial(main_kernel, count), out_shape=outs, in_...  22.8 us
    pallas_call x1, Pallas kernels, shards(): pl.pallas_call(store_kernel, out_shape=outs, in_specs=[pl.BlockSpec(memor...  1.07 us

profile of v12, /device:TPU:57, one launch (start us, length us, event | category | flops | bytes accessed | tf_op | source)
XLA Modules:
  0.0 24.5 jit_solution(7092328061321232988)
XLA Ops:
  0.6 22.8 %attend.1 = (bf16[2,128,1024]{2,1,0:T(8,128)(2,1)S(1)}, bf16[2,128,1024]{2,1,0:T(8,128)(2,1)S(1)}, bf16[2,128,128]{2,1,0:T(8,128)(2,1)S(1)}, bf16[2,128,128]{2,1,0:T(8,128)(2,1)S(1)}) custom-call(bf16[2,128,1024]{2,1,0:T(8,128)(2,1)} %bitcast.9, bf16[2,128,1024]{2,1,0:T(8,128)(2,1)} %bitcast.10, bf16[2,128,128]{2,1,0:T(8,128)(2,1)} %bitcast.11, ...), custom_call_target="tpu_custom_call" | custom-call | tf_op jit(solution)/shard_map/attend/pallas_call | solution.py:443
  23.4 1.1 %store.1 = (bf16[2,128,1024]{2,1,0:T(8,128)(2,1)}, bf16[2,128,1024]{2,1,0:T(8,128)(2,1)}, bf16[2,128,128]{2,1,0:T(8,128)(2,1)}, bf16[2,128,128]{2,1,0:T(8,128)(2,1)}) custom-call(bf16[2,128,1024]{2,1,0:T(8,128)(2,1)S(1)} %get-tuple-element.12.refs_0_, bf16[2,128,1024]{2,1,0:T(8,128)(2,1)S(1)} %get-tuple-element.13.refs_1_, ...), custom_call_target="tpu_custom_call" | custom-call | tf_op jit(solution)/shard_map/store/pallas_call | solution.py:509

commit v13 on v12

--- a/solution.py
+++ b/solution.py
@@ -47,7 +47,7 @@
 def main_kernel(
     count, q, g, k, v, lens, assign, attn, dq, dk, dv,
     lens_v, assign_s, padded, qslot, gslot, kown, vown, kprev, vprev, qr, gr, qt, gt,
-    ko, vo, kot, vot, kp, vp, kpt, vpt, bias, expo, dpo, pb, sb, oto, stat,
+    ko, vo, vot, kp, vp, vpt, bias, expo, dpo, pb, sb, oto, stat,
     part_p, part_o, sum_send, sum_near, far_send_buf, far_buf, own_send, own_near,
     o_mine, o_send, o_near, q_mine, q_send, q_near,
     arrived, loc_sem, far_ks, far_kr, far_vs, far_vr, rel_ks, rel_kr, rel_vs, rel_vr,
@@ -106,7 +106,7 @@
     def _():
         pl.semaphore_signal(barrier, inc=1, device_id=(before, grp), device_id_type=MESH)
 
-    for copy in local:
+    for copy in local[:4]:
         copy.start()
     pl.semaphore_wait(barrier, 1 + has_next.astype(jnp.int32))
 
@@ -116,7 +116,7 @@
         for copy in far_k + far_v:
             copy.start()
 
-    for copy in near[:2]:
+    for copy in near[:2] + local[4:]:
         copy.start()
 
     docs = lens_v.shape[0]
@@ -166,7 +166,6 @@
         vb = vown[slot]
         ko[rows] = kb
         vo[rows] = vb
-        kot[:, rows] = kb.T
         vot[:, rows] = vb.T
         qb = qslot[slot]
         gb = gslot[slot]
@@ -191,15 +190,20 @@
             top = fold(piece, jnp.max) if top is None else jnp.maximum(top, fold(piece, jnp.max))
         return jnp.max(top, axis=0, keepdims=True)
 
-    def exponentials(j, first, n, top, low=None):
-        total = None
+    def exponentials(j, first, n, top):
+        total = jnp.zeros((8, width), F32)
         for at in range(0, n, PIECE):
             rows = slice(first + at, first + at + PIECE)
             e = jnp.exp2(expo[j, rows] - top)
             expo[j, rows] = e
-            if low is not None:
-                low[j, rows] = e.astype(BF16)
-            total = fold(e, jnp.sum) if total is None else total + fold(e, jnp.sum)
+            total = total + fold(e, jnp.sum)
+        return jnp.sum(total, axis=0, keepdims=True)
+
+    def weighted(j, first, dp):
+        total = jnp.zeros((8, width), F32)
+        for at in range(0, dp.shape[0], PIECE):
+            rows = slice(first + at, first + at + PIECE)
+            total = total + fold(expo[j, rows] * dp[at : at + PIECE], jnp.sum)
         return jnp.sum(total, axis=0, keepdims=True)
 
     tops = []
@@ -210,8 +214,9 @@
     for j in range(GROUP):
         n = (j + 1) * SPAN
         stat[j, 0:1] = tops[j]
-        stat[j, 1:2] = exponentials(j, 0, n, tops[j], pb)
-        oto[j] = dot(vot[:, 0:n], pb[j, 0:n], NN)
+        stat[j, 1:2] = exponentials(j, 0, n, tops[j])
+        stat[j, 2:3] = weighted(j, 0, dpo[j, 0:n])
+        oto[j] = dot(vot[:, 0:n], expo[j, 0:n].astype(BF16), NN)
 
     @pl.when(has_prev)
     def _():
@@ -231,7 +236,6 @@
         rows = slice(i * SPAN, (i + 1) * SPAN)
         kb = kprev[pick(there, i)]
         kp[rows] = kb
-        kpt[:, rows] = kb.T
 
     tops = []
     for j in range(GROUP):
@@ -253,13 +257,6 @@
                     far_v[a].wait_recv()
                     relay_v[a].start()
 
-    for j in range(GROUP):
-        for at in range((j + 1) * SPAN, expo.shape[1], PIECE):
-            rows = slice(at, at + PIECE)
-            pr = expo[j, rows] * norms[j]
-            expo[j, rows] = pr
-            pb[j, rows] = pr.astype(BF16)
-
     @pl.when(has_prev)
     def _():
         for a in range(2):
@@ -269,57 +266,62 @@
         rows = slice(i * SPAN, (i + 1) * SPAN)
         vb = vprev[pick(there, i)]
         vp[rows] = vb
-        vpt[:, rows] = vb.T
 
     deltas = []
 
-    def finish_out(j):
+    def prev_grads(j, dp):
+        at = (j + 1) * SPAN
+        delta = alphas[j] * stat[j, 2:3] + norms[j] * weighted(j, at, dp)
+        deltas.append(delta)
+        for p in range(0, dp.shape[0], PIECE):
+            rows = slice(at + p, at + p + PIECE)
+            pr = expo[j, rows] * norms[j]
+            pb[j, rows] = pr.astype(BF16)
+            sb[j, rows] = (pr * (dp[p : p + PIECE] - delta)).astype(BF16)
+        part_p[j:, :, 0:DIM] += spans(dot(sb[j, at:], qr[j], NN) * ROOT)
+        part_p[j:, :, DIM:] += spans(dot(pb[j, at:], gr[j], NN))
+
+    dp = dot(vp[...], gt[0], NN)
+    for j in range(GROUP):
+        next_dp = dot(vp[(j + 1) * SPAN :], gt[j + 1], NN) if j < GROUP - 1 else None
+        prev_grads(j, dp)
+        dp = next_dp
+
+    def mine_of(spans, a):
+        return jnp.where(core == 0, spans[a], spans[2 + a])
+
+    def theirs_of(spans, a):
+        return jnp.where(core == 0, spans[2 + a], spans[a])
+
+    swap_p = [remote(sum_send.at[a], sum_near.at[a], p_s.at[a], p_r.at[a], beside)
+              for a in range(2)]
+    far_p = [remote(far_send_buf.at[a], far_buf.at[a], f_s.at[a], f_r.at[a], before)
+             for a in range(2)]
+    for a in range(2):
+        sum_send[a] = part_p[theirs_of(there, a)].astype(BF16)
+        swap_p[a].start()
+
+    swap_out = remote(o_send, o_near, oq_s.at[0], oq_r.at[0], beside)
+    swap_dq = remote(q_send, q_near, oq_s.at[1], oq_r.at[1], beside)
+    vpt[...] = vp[...].T
+    for j in range(GROUP):
         out = oto[j] * alphas[j] + dot(vpt[:, j * SPAN :], pb[j, (j + 1) * SPAN :], NN)
-        deltas.append(jnp.sum(out * gt[j].astype(F32), axis=0, keepdims=True))
         out = out.astype(BF16)
         for h in range(heads):
             cols = slice(h * DIM, (h + 1) * DIM)
             o_mine[j, :, cols] = out[:, cols].T
-
-    def prev_dprobs(j):
-        return dot(vp[j * SPAN :], gt[j], NN)
-
-    def prev_grads(j, dp):
-        at = (j + 1) * SPAN
-        for p in range(0, dp.shape[0], PIECE):
-            rows = slice(at + p, at + p + PIECE)
-            sb[j, rows] = (expo[j, rows] * (dp[p : p + PIECE] - deltas[j])).astype(BF16)
-        part_p[j:, :, 0:DIM] += spans(dot(sb[j, at:], qr[j], NN) * ROOT)
-        part_p[j:, :, DIM:] += spans(dot(pb[j, at:], gr[j], NN))
-
-    finish_out(0)
-    dp = prev_dprobs(0)
-    for j in range(1, GROUP):
-        finish_out(j)
-        next_dp = prev_dprobs(j)
-        prev_grads(j - 1, dp)
-        dp = next_dp
-    prev_grads(GROUP - 1, dp)
-
-    def mine_of(spans, a):
-        return jnp.where(core == 0, spans[a], spans[2 + a])
-
-    def theirs_of(spans, a):
-        return jnp.where(core == 0, spans[2 + a], spans[a])
-
-    swap_p = [remote(sum_send.at[a], sum_near.at[a], p_s.at[a], p_r.at[a], beside)
-              for a in range(2)]
-    far_p = [remote(far_send_buf.at[a], far_buf.at[a], f_s.at[a], f_r.at[a], before)
-             for a in range(2)]
-    for a in range(2):
-        sum_send[a] = part_p[theirs_of(there, a)].astype(BF16)
-        swap_p[a].start()
-
-    swap_out = remote(o_send, o_near, oq_s.at[0], oq_r.at[0], beside)
-    swap_dq = remote(q_send, q_near, oq_s.at[1], oq_r.at[1], beside)
     for a in range(2):
         o_send[a] = o_mine[theirs_of(here, a)]
     swap_out.start()
+
+    for a in range(2):
+        swap_p[a].wait_recv()
+        far_send_buf[a] = (
+            part_p[mine_of(there, a)] + sum_near[a].astype(F32)).astype(BF16)
+
+        @pl.when(has_prev)
+        def _(a=a):
+            far_p[a].start()
 
     def own_dscores(j):
         for at in range(0, (j + 1) * SPAN, PIECE):
@@ -350,15 +352,6 @@
     for a in range(2):
         q_send[a] = q_mine[theirs_of(here, a)]
     swap_dq.start()
-
-    for a in range(2):
-        swap_p[a].wait_recv()
-        far_send_buf[a] = (
-            part_p[mine_of(there, a)] + sum_near[a].astype(F32)).astype(BF16)
-
-        @pl.when(has_prev)
-        def _(a=a):
-            far_p[a].start()
 
     for j in range(GROUP):
         own_grads(j)
@@ -462,10 +455,8 @@
             pltpu.VMEM((keyed, DIM), BF16),
             pltpu.VMEM((keyed, DIM), BF16),
             pltpu.VMEM((DIM, keyed), BF16),
-            pltpu.VMEM((DIM, keyed), BF16),
             pltpu.VMEM((keyed, DIM), BF16),
             pltpu.VMEM((keyed, DIM), BF16),
-            pltpu.VMEM((DIM, keyed), BF16),
             pltpu.VMEM((DIM, keyed), BF16),
             pltpu.VMEM((GROUP, seen, SPAN), F32),
             pltpu.VMEM((GROUP, seen, half), F32),

time: 24.8 us -> 25.1 us (1.012)
  Pallas kernels: 23.9 us -> 24.3 us
    pallas_call x1, Pallas kernels: 22.8 us -> 23.2 us  [shards(): pl.pallas_call(functools.partial(main_kernel, count), out_shape=outs, in_...]
where the time goes in v13:
time: 25.1 us; the launch traced here: 24.9 us
  Pallas kernels  24.3 us (97%)
  between operations  0.64 us (3%)
    pallas_call x1, Pallas kernels, shards(): pl.pallas_call(functools.partial(main_kernel, count), out_shape=outs, in_...  23.2 us
    pallas_call x1, Pallas kernels, shards(): pl.pallas_call(store_kernel, out_shape=outs, in_specs=[pl.BlockSpec(memor...  1.07 us

profile of v13, /device:TPU:57, one launch (start us, length us, event | category | flops | bytes accessed | tf_op | source)
XLA Modules:
  0.0 24.9 jit_solution(15657962276491371116)
XLA Ops:
  0.6 23.2 %attend.1 = (bf16[2,128,1024]{2,1,0:T(8,128)(2,1)S(1)}, bf16[2,128,1024]{2,1,0:T(8,128)(2,1)S(1)}, bf16[2,128,128]{2,1,0:T(8,128)(2,1)S(1)}, bf16[2,128,128]{2,1,0:T(8,128)(2,1)S(1)}) custom-call(bf16[2,128,1024]{2,1,0:T(8,128)(2,1)} %bitcast.9, bf16[2,128,1024]{2,1,0:T(8,128)(2,1)} %bitcast.10, bf16[2,128,128]{2,1,0:T(8,128)(2,1)} %bitcast.11, ...), custom_call_target="tpu_custom_call" | custom-call | tf_op jit(solution)/shard_map/attend/pallas_call | solution.py:436
  23.9 1.1 %store.1 = (bf16[2,128,1024]{2,1,0:T(8,128)(2,1)}, bf16[2,128,1024]{2,1,0:T(8,128)(2,1)}, bf16[2,128,128]{2,1,0:T(8,128)(2,1)}, bf16[2,128,128]{2,1,0:T(8,128)(2,1)}) custom-call(bf16[2,128,1024]{2,1,0:T(8,128)(2,1)S(1)} %get-tuple-element.12.refs_0_, bf16[2,128,1024]{2,1,0:T(8,128)(2,1)S(1)} %get-tuple-element.13.refs_1_, ...), custom_call_target="tpu_custom_call" | custom-call | tf_op jit(solution)/shard_map/store/pallas_call | solution.py:500

commit v14 on v12

--- a/solution.py
+++ b/solution.py
@@ -106,17 +106,17 @@
     def _():
         pl.semaphore_signal(barrier, inc=1, device_id=(before, grp), device_id_type=MESH)
 
-    for copy in local:
+    for copy in local[:4]:
         copy.start()
     pl.semaphore_wait(barrier, 1 + has_next.astype(jnp.int32))
 
     @pl.when(has_next)
     def _():
         pl.semaphore_signal(arrived, inc=1, device_id=(after, grp), device_id_type=MESH)
-        for copy in far_k + far_v:
+        for copy in far_k:
             copy.start()
 
-    for copy in near[:2]:
+    for copy in near[:2] + local[4:]:
         copy.start()
 
     docs = lens_v.shape[0]
@@ -139,6 +139,13 @@
     key_row = lax.broadcasted_iota(jnp.int32, (SPAN, SPAN), 0).astype(F32)
     query_col = lax.broadcasted_iota(jnp.int32, (SPAN, SPAN), 1).astype(F32)
     for j in range(GROUP):
+        if j == 2:
+
+            @pl.when(has_next)
+            def _():
+                for copy in far_v:
+                    copy.start()
+
         pos = query_col[0:1] + float(j * SPAN)
         start = jnp.max(jnp.where(ends <= pos, ends, least), axis=0, keepdims=True)
         for b in range(GROUP + 1):

time: 24.8 us -> 24.8 us (level)
  no operation moved by 1% of the time
where the time goes in v14:
time: 24.8 us; the launch traced here: 24.5 us
  Pallas kernels  23.9 us (96%)
  between operations  0.64 us (3%)
    pallas_call x1, Pallas kernels, shards(): pl.pallas_call(functools.partial(main_kernel, count), out_shape=outs, in_...  22.8 us
    pallas_call x1, Pallas kernels, shards(): pl.pallas_call(store_kernel, out_shape=outs, in_specs=[pl.BlockSpec(memor...  1.07 us

profile of v14, /device:TPU:57, one launch (start us, length us, event | category | flops | bytes accessed | tf_op | source)
XLA Modules:
  0.0 24.5 jit_solution(13531198041678986861)
XLA Ops:
  0.6 22.8 %attend.1 = (bf16[2,128,1024]{2,1,0:T(8,128)(2,1)S(1)}, bf16[2,128,1024]{2,1,0:T(8,128)(2,1)S(1)}, bf16[2,128,128]{2,1,0:T(8,128)(2,1)S(1)}, bf16[2,128,128]{2,1,0:T(8,128)(2,1)S(1)}) custom-call(bf16[2,128,1024]{2,1,0:T(8,128)(2,1)} %bitcast.9, bf16[2,128,1024]{2,1,0:T(8,128)(2,1)} %bitcast.10, bf16[2,128,128]{2,1,0:T(8,128)(2,1)} %bitcast.11, ...), custom_call_target="tpu_custom_call" | custom-call | tf_op jit(solution)/shard_map/attend/pallas_call | solution.py:450
  23.4 1.1 %store.1 = (bf16[2,128,1024]{2,1,0:T(8,128)(2,1)}, bf16[2,128,1024]{2,1,0:T(8,128)(2,1)}, bf16[2,128,128]{2,1,0:T(8,128)(2,1)}, bf16[2,128,128]{2,1,0:T(8,128)(2,1)}) custom-call(bf16[2,128,1024]{2,1,0:T(8,128)(2,1)S(1)} %get-tuple-element.12.refs_0_, bf16[2,128,1024]{2,1,0:T(8,128)(2,1)S(1)} %get-tuple-element.13.refs_1_, ...), custom_call_target="tpu_custom_call" | custom-call | tf_op jit(solution)/shard_map/store/pallas_call | solution.py:516

commit v15 on v14

--- a/solution.py
+++ b/solution.py
@@ -267,6 +267,16 @@
             expo[j, rows] = pr
             pb[j, rows] = pr.astype(BF16)
 
+    for j in range(GROUP):
+        own = slice(0, (j + 1) * SPAN)
+        part_p[j:, :, DIM:] += spans(dot(pb[j, (j + 1) * SPAN :], gr[j], NN))
+        for at in range(0, (j + 1) * SPAN, PIECE):
+            rows = slice(at, at + PIECE)
+            pr = expo[j, rows] * alphas[j]
+            expo[j, rows] = pr
+            pb[j, rows] = pr.astype(BF16)
+        part_o[0 : j + 1, :, DIM:] += spans(dot(pb[j, own], gr[j], NN))
+
     @pl.when(has_prev)
     def _():
         for a in range(2):
@@ -297,7 +307,6 @@
             rows = slice(at + p, at + p + PIECE)
             sb[j, rows] = (expo[j, rows] * (dp[p : p + PIECE] - deltas[j])).astype(BF16)
         part_p[j:, :, 0:DIM] += spans(dot(sb[j, at:], qr[j], NN) * ROOT)
-        part_p[j:, :, DIM:] += spans(dot(pb[j, at:], gr[j], NN))
 
     finish_out(0)
     dp = prev_dprobs(0)
@@ -331,9 +340,7 @@
     def own_dscores(j):
         for at in range(0, (j + 1) * SPAN, PIECE):
             rows = slice(at, at + PIECE)
-            pr = expo[j, rows] * alphas[j]
-            pb[j, rows] = pr.astype(BF16)
-            sb[j, rows] = (pr * (dpo[j, rows] - deltas[j])).astype(BF16)
+            sb[j, rows] = (expo[j, rows] * (dpo[j, rows] - deltas[j])).astype(BF16)
 
     def query_grads(j):
         own = slice(0, (j + 1) * SPAN)
@@ -347,7 +354,6 @@
     def own_grads(j):
         own = slice(0, (j + 1) * SPAN)
         part_o[0 : j + 1, :, 0:DIM] += spans(dot(sb[j, own], qr[j], NN) * ROOT)
-        part_o[0 : j + 1, :, DIM:] += spans(dot(pb[j, own], gr[j], NN))
 
     own_dscores(0)
     for j in range(1, GROUP):

time: 24.8 us -> 24.9 us (level)
  no operation moved by 1% of the time
where the time goes in v15:
time: 24.9 us; the launch traced here: 24.7 us
  Pallas kernels  24 us (96%)
  between operations  0.64 us (3%)
    pallas_call x1, Pallas kernels, shards(): pl.pallas_call(functools.partial(main_kernel, count), out_shape=outs, in_...  23 us
    pallas_call x1, Pallas kernels, shards(): pl.pallas_call(store_kernel, out_shape=outs, in_specs=[pl.BlockSpec(memor...  1.07 us

profile of v15, /device:TPU:57, one launch (start us, length us, event | category | flops | bytes accessed | tf_op | source)
XLA Modules:
  0.0 24.7 jit_solution(11046186978112048640)
XLA Ops:
  0.6 23.0 %attend.1 = (bf16[2,128,1024]{2,1,0:T(8,128)(2,1)S(1)}, bf16[2,128,1024]{2,1,0:T(8,128)(2,1)S(1)}, bf16[2,128,128]{2,1,0:T(8,128)(2,1)S(1)}, bf16[2,128,128]{2,1,0:T(8,128)(2,1)S(1)}) custom-call(bf16[2,128,1024]{2,1,0:T(8,128)(2,1)} %bitcast.9, bf16[2,128,1024]{2,1,0:T(8,128)(2,1)} %bitcast.10, bf16[2,128,128]{2,1,0:T(8,128)(2,1)} %bitcast.11, ...), custom_call_target="tpu_custom_call" | custom-call | tf_op jit(solution)/shard_map/attend/pallas_call | solution.py:456
  23.6 1.1 %store.1 = (bf16[2,128,1024]{2,1,0:T(8,128)(2,1)}, bf16[2,128,1024]{2,1,0:T(8,128)(2,1)}, bf16[2,128,128]{2,1,0:T(8,128)(2,1)}, bf16[2,128,128]{2,1,0:T(8,128)(2,1)}) custom-call(bf16[2,128,1024]{2,1,0:T(8,128)(2,1)S(1)} %get-tuple-element.12.refs_0_, bf16[2,128,1024]{2,1,0:T(8,128)(2,1)S(1)} %get-tuple-element.13.refs_1_, ...), custom_call_target="tpu_custom_call" | custom-call | tf_op jit(solution)/shard_map/store/pallas_call | solution.py:522

commit v16 on v14

--- a/solution.py
+++ b/solution.py
@@ -350,13 +350,9 @@
         part_o[0 : j + 1, :, DIM:] += spans(dot(pb[j, own], gr[j], NN))
 
     own_dscores(0)
-    for j in range(1, GROUP):
+    for j in range(1, GROUP - 1):
         own_dscores(j)
         query_grads(j - 1)
-    query_grads(GROUP - 1)
-    for a in range(2):
-        q_send[a] = q_mine[theirs_of(here, a)]
-    swap_dq.start()
 
     for a in range(2):
         swap_p[a].wait_recv()
@@ -366,6 +362,13 @@
         @pl.when(has_prev)
         def _(a=a):
             far_p[a].start()
+
+    own_dscores(GROUP - 1)
+    query_grads(GROUP - 2)
+    query_grads(GROUP - 1)
+    for a in range(2):
+        q_send[a] = q_mine[theirs_of(here, a)]
+    swap_dq.start()
 
     for j in range(GROUP):
         own_grads(j)

time: 24.8 us -> 24.9 us (level)
  no operation moved by 1% of the time
where the time goes in v16:
time: 24.9 us; the launch traced here: 24.7 us
  Pallas kernels  24.1 us (97%)
  between operations  0.64 us (3%)
    pallas_call x1, Pallas kernels, shards(): pl.pallas_call(functools.partial(main_kernel, count), out_shape=outs, in_...  23 us
    pallas_call x1, Pallas kernels, shards(): pl.pallas_call(store_kernel, out_shape=outs, in_specs=[pl.BlockSpec(memor...  1.07 us

profile of v16, /device:TPU:57, one launch (start us, length us, event | category | flops | bytes accessed | tf_op | source)
XLA Modules:
  0.0 24.7 jit_solution(13847540481922614668)
XLA Ops:
  0.6 23.0 %attend.1 = (bf16[2,128,1024]{2,1,0:T(8,128)(2,1)S(1)}, bf16[2,128,1024]{2,1,0:T(8,128)(2,1)S(1)}, bf16[2,128,128]{2,1,0:T(8,128)(2,1)S(1)}, bf16[2,128,128]{2,1,0:T(8,128)(2,1)S(1)}) custom-call(bf16[2,128,1024]{2,1,0:T(8,128)(2,1)} %bitcast.9, bf16[2,128,1024]{2,1,0:T(8,128)(2,1)} %bitcast.10, bf16[2,128,128]{2,1,0:T(8,128)(2,1)} %bitcast.11, ...), custom_call_target="tpu_custom_call" | custom-call | tf_op jit(solution)/shard_map/attend/pallas_call | solution.py:453
  23.7 1.1 %store.1 = (bf16[2,128,1024]{2,1,0:T(8,128)(2,1)}, bf16[2,128,1024]{2,1,0:T(8,128)(2,1)}, bf16[2,128,128]{2,1,0:T(8,128)(2,1)}, bf16[2,128,128]{2,1,0:T(8,128)(2,1)}) custom-call(bf16[2,128,1024]{2,1,0:T(8,128)(2,1)S(1)} %get-tuple-element.12.refs_0_, bf16[2,128,1024]{2,1,0:T(8,128)(2,1)S(1)} %get-tuple-element.13.refs_1_, ...), custom_call_target="tpu_custom_call" | custom-call | tf_op jit(solution)/shard_map/store/pallas_call | solution.py:519

commit v17 on v14

--- a/solution.py
+++ b/solution.py
@@ -139,7 +139,7 @@
     key_row = lax.broadcasted_iota(jnp.int32, (SPAN, SPAN), 0).astype(F32)
     query_col = lax.broadcasted_iota(jnp.int32, (SPAN, SPAN), 1).astype(F32)
     for j in range(GROUP):
-        if j == 2:
+        if j == 1:
 
             @pl.when(has_next)
             def _():

time: 24.8 us -> 24.8 us (level)
  no operation moved by 1% of the time
where the time goes in v17:
time: 24.8 us; the launch traced here: 24.5 us
  Pallas kernels  23.8 us (96%)
  between operations  0.64 us (3%)
    pallas_call x1, Pallas kernels, shards(): pl.pallas_call(functools.partial(main_kernel, count), out_shape=outs, in_...  22.8 us
    pallas_call x1, Pallas kernels, shards(): pl.pallas_call(store_kernel, out_shape=outs, in_specs=[pl.BlockSpec(memor...  1.07 us

profile of v17, /device:TPU:57, one launch (start us, length us, event | category | flops | bytes accessed | tf_op | source)
XLA Modules:
  0.0 24.5 jit_solution(12396887214379972638)
XLA Ops:
  0.6 22.8 %attend.1 = (bf16[2,128,1024]{2,1,0:T(8,128)(2,1)S(1)}, bf16[2,128,1024]{2,1,0:T(8,128)(2,1)S(1)}, bf16[2,128,128]{2,1,0:T(8,128)(2,1)S(1)}, bf16[2,128,128]{2,1,0:T(8,128)(2,1)S(1)}) custom-call(bf16[2,128,1024]{2,1,0:T(8,128)(2,1)} %bitcast.9, bf16[2,128,1024]{2,1,0:T(8,128)(2,1)} %bitcast.10, bf16[2,128,128]{2,1,0:T(8,128)(2,1)} %bitcast.11, ...), custom_call_target="tpu_custom_call" | custom-call | tf_op jit(solution)/shard_map/attend/pallas_call | solution.py:450
  23.4 1.1 %store.1 = (bf16[2,128,1024]{2,1,0:T(8,128)(2,1)}, bf16[2,128,1024]{2,1,0:T(8,128)(2,1)}, bf16[2,128,128]{2,1,0:T(8,128)(2,1)}, bf16[2,128,128]{2,1,0:T(8,128)(2,1)}) custom-call(bf16[2,128,1024]{2,1,0:T(8,128)(2,1)S(1)} %get-tuple-element.12.refs_0_, bf16[2,128,1024]{2,1,0:T(8,128)(2,1)S(1)} %get-tuple-element.13.refs_1_, ...), custom_call_target="tpu_custom_call" | custom-call | tf_op jit(solution)/shard_map/store/pallas_call | solution.py:516
